TPU v7x, 256 devices: a whole 4x4x8 slice. The times are simulated.
256 devices in a mesh: col: 64 (over z, x, core), row: 4 (over y).
Axes of the slice: x: 4, y: 4, z: 8, core: 2. Of those that a mesh axis runs over, the one named last changes fastest.
Arguments:
- amplitudes: bfloat16 [16, 512, 512], P(None, 'col', 'row'), may hold values from -6 to 6
- integrals: bfloat16 [32768, 32768], P('col', 'row'), may hold values from -0.03125 to 0.03125
- partner: int32 [8], replicated, may hold values from 0 to 7, as said below
Outputs:
- ladder: bfloat16 [16, 512, 512], P(None, 'col', 'row')
Inputs may be any that keep to these rules, and one draw needn't show every extreme that they name: partner is an involution without fixed points: tile d pairs with the tile whose irrep times d's irrep is the occupied pairs' irrep.
All inputs are finite; a program needn't handle non-finite values.
Results may differ from a plain program's by a relative error of at most 0.001.
Values may be sent and summed in bfloat16 or wider, within the bound.
No kernel may reach another device: no remote copies, remote signals or barrier semaphores. Data moves between devices by JAX's collectives and lax.ppermute only.
A program may use at most 64 MiB of HBM per device.

v0:
```python
import jax
import jax.numpy as jnp
from jax import lax
from jax.sharding import PartitionSpec as P

TS = 64


def lookup(table, which):
    count = table.shape[0]
    hits = jnp.arange(count, dtype=jnp.int32)[None, :] == which[:, None]
    return jnp.sum(jnp.where(hits, table[None, :], 0), axis=1)


def per_device(amplitudes, integrals, partner):
    n_col = lax.axis_size("col")
    n_row = lax.axis_size("row")
    pairs = amplitudes.shape[0]
    rows_dev = amplitudes.shape[1]
    cols_dev = amplitudes.shape[2]
    tiles = rows_dev * n_col // TS
    group = tiles // n_row
    per_tile = n_col // tiles
    col_id = lax.axis_index("col")
    row_id = lax.axis_index("row")
    ket_tiles = row_id * group + jnp.arange(group, dtype=jnp.int32)
    source_tiles = lookup(partner, ket_tiles)
    gathered = lax.all_gather(amplitudes, "col", axis=1, tiled=True)
    pieces = []
    for slot in range(group):
        start_row = source_tiles[slot] * TS
        pieces.append(
            lax.dynamic_slice(
                gathered, (jnp.int32(0), start_row, jnp.int32(slot * TS)), (pairs, TS, TS)
            )
        )
    packed = jnp.stack(pieces, 1).reshape(pairs, group * TS * TS)
    partial_sum = lax.dot_general(
        packed, integrals, (((1,), (1,)), ((), ())), preferred_element_type=jnp.float32
    )
    finished = lax.psum(partial_sum, "row").astype(jnp.bfloat16)
    bra_tile = col_id // per_tile
    row_offset = col_id % per_tile * rows_dev
    ket_tile = lookup(partner, bra_tile[None])[0]
    every_block = lax.all_gather(finished, "col", axis=1, tiled=True)
    every_block = every_block.reshape(pairs, tiles, TS, TS)
    chosen = lax.dynamic_slice(
        every_block, (jnp.int32(0), ket_tile, row_offset, jnp.int32(0)), (pairs, 1, rows_dev, TS)
    )
    chosen = chosen.reshape(pairs, rows_dev, TS)
    keep = (ket_tile // group == row_id).astype(jnp.bfloat16)
    chosen = chosen * keep
    output = jnp.zeros((pairs, rows_dev, cols_dev), jnp.bfloat16)
    column_start = ket_tile % group * TS
    return lax.dynamic_update_slice(output, chosen, (jnp.int32(0), jnp.int32(0), column_start))


def solution(mesh):
    return jax.shard_map(
        per_device,
        mesh=mesh,
        in_specs=(P(None, "col", "row"), P("col", "row"), P()),
        out_specs=P(None, "col", "row"),
        check_vma=False,
    )
```

profile of v0, /device:TPU:16, one launch (start us, length us, event | category | flops | bytes accessed | tf_op | source)
XLA Modules:
  0.0 190.2 jit_solution(17744023053151767164)
XLA Ops:
  6.5 0.0 copy-start
  6.5 0.0 all-gather.3.cloned.1.call-start
  6.5 0.7 all-gather.3.cloned.1.call-update
  7.3 0.0 all-gather.5.cloned.1.call-start
  7.3 0.8 fusion.1
  8.2 0.6 fusion.3
  10.0 75.3 %all-gather.3.cloned.1.call-done = bf16[16,512,128]{2,1,0:T(8,128)(2,1)} async-done(((bf16[16,8,128]{2,1,0:T(8,128)(2,1)}), bf16[16,512,128]{2,1,0:T(8,128)(2,1)}) %all-gather.3.cloned.1.call-update) | async-done | bytes 2097168 | tf_op jit(solution)/shard_map/all_gather | solution.py:28
  85.3 1.2 dynamic-slice_bitcast_fusion.1
  86.5 0.1 pad_maximum_fusion
  86.6 0.5 reshape.26
  87.1 5.6 %fusion.4 = f32[16,512]{1,0:T(8,128)S(1)} fusion(bf16[16,8192]{1,0:T(8,128)(2,1)S(1)} %reshape.26, bf16[512,8192]{1,0:T(8,128)(2,1)} %param.4), kind=kOutput, calls=%fused_computation.11 | convolution fusion | flops 134217728 | bytes 8683520 | tf_op jit(solution)/shard_map/dot_general | solution.py:38
  92.7 16.1 %psum.7 = bf16[16,512]{1,0:T(8,128)(2,1)} all-reduce(f32[16,512]{1,0:T(8,128)S(1)} %fusion.4), channel_id=1, replica_groups=mesh['col'=64,'row'=4] {'row'}, use_global_device_ids=true, to_apply=%region_1.2 | all-reduce | flops 8192 | bytes 49152 | tf_op jit(solution)/shard_map/psum | solution.py:41
  108.8 0.0 all-gather.5.cloned.1.call-update
  108.8 0.0 copy-done
  108.9 0.6 fusion.2
  112.9 65.3 %all-gather.5.cloned.1.call-done = bf16[16,32768]{1,0:T(8,128)(2,1)} async-done(((bf16[16,512]{1,0:T(8,128)(2,1)}), bf16[16,32768]{1,0:T(8,128)(2,1)}) %all-gather.5.cloned.1.call-update) | async-done | bytes 1048592 | tf_op jit(solution)/shard_map/all_gather | solution.py:45
  178.3 3.0 %reshape.27 = bf16[16,8,64,64]{3,2,1,0:T(8,128)(2,1)S(1)} reshape(bf16[16,32768]{1,0:T(8,128)(2,1)} %all-gather.5.cloned.1.call-done) | data formatting | bytes 2097152 | tf_op jit(solution)/shard_map/reshape | solution.py:46
  181.3 0.6 broadcast_in_dim.24
  181.9 1.5 dynamic_update_slice.3
  (2 shorter events, 0.0 us)
Async XLA Ops:
  6.5 102.3 %copy-start = (s32[8]{0:T(128)S(1)}, s32[8]{0:T(128)}, u32[]{:S(2)}) copy-start(s32[8]{0:T(128)} %param.5) | copy-start | bytes 100
  6.5 78.8 %all-gather.3.cloned.1.call-start = ((), (), s32[]{:S(2)}) async-start(), calls=%async_computation | async-start | bytes 2129920 | tf_op jit(solution)/shard_map/all_gather | solution.py:28
  7.3 171.0 %all-gather.5.cloned.1.call-start = ((), (), s32[]{:S(2)}) async-start(), calls=%async_computation.1 | async-start | bytes 1064960 | tf_op jit(solution)/shard_map/all_gather | solution.py:45
Sparse Core Ops, SparseCore 0:
  10.0 75.2 all-gather.2
  109.0 69.2 all-gather.4
where the time goes:
time: 192 us; the launch traced here: 190 us
  waiting for transfers between devices  141 us (73%)
  between operations  18.2 us (9%)
  blocking collectives  16.1 us (8%)
  local copies, waits for them, and re-layouts  7.37 us (4%)
  matrix products  5.65 us (3%)
    all_gather x1, waiting for transfers between devices, per_device(): gathered = lax.all_gather(amplitudes, 'col', axis=1, tiled=True)  75.3 us
    all_gather x1, waiting for transfers between devices, per_device(): every_block = lax.all_gather(finished, 'col', axis=1, tiled=True)  65.3 us
    psum x1, blocking collectives, per_device(): finished = lax.psum(partial_sum, 'row').astype(jnp.bfloat16)  16.1 us
    dot_general x1, matrix products, per_device(): lax.dot_general(packed, integrals, (((1,), (1,)), ((), ())), preferred_el...  5.65 us
  transfers between devices with their start and end apart: 2, of which 2 were waited for; matrix products, arithmetic and copies ran while one was open for 1% of the time, Pallas kernels for 0%

commit v1 on v0

v1 whole, which is shorter than its diff:
```python
import jax
import jax.numpy as jnp
from jax import lax
from jax.experimental import pallas as pl
from jax.experimental.pallas import tpu as pltpu
from jax.sharding import Mesh
from jax.sharding import PartitionSpec as P

TS = 64
ZH, ZL, X, CORE, ROW = 4, 2, 4, 2, 4
AXES = ("zh", "zl", "x", "core", "row")
REACH = (3, 1, 0, 2)


def target_z(zh, zl, row):
    off = REACH[(row - zh) % ROW]
    return (2 * zh - off) % (ZH * ZL) if zl == 0 else (2 * zh + 1 + off) % (ZH * ZL)


def linear(zh, zl, x, core, row):
    return (((zh * ZL + zl) * X + x) * CORE + core) * ROW + row


def delivery_pairs():
    pairs = []
    for zh in range(ZH):
        for zl in range(ZL):
            for x in range(X):
                for core in range(CORE):
                    for row in range(ROW):
                        t = target_z(zh, zl, row)
                        pairs.append((linear(zh, zl, x, core, row), linear(t // ZL, t % ZL, x, core, zh)))
    return pairs


def matmul_kernel(packed_ref, integrals_ref, out_ref):
    subs, halves, pairs, width = packed_ref.shape
    half_width = subs * width
    total = jnp.zeros((pairs, integrals_ref.shape[0]), jnp.float32)
    for h in range(halves):
        for s in range(subs):
            total = total + lax.dot_general(
                packed_ref[s, h],
                integrals_ref[:, pl.ds(h * half_width + s * width, width)],
                (((1,), (1,)), ((), ())),
                preferred_element_type=jnp.float32,
            )
    for j in range(out_ref.shape[0]):
        out_ref[j] = total


def per_device(amplitudes, integrals, partner):
    zh, zl = lax.axis_index("zh"), lax.axis_index("zl")
    row = lax.axis_index("row")
    z = zh * ZL + zl
    pairs, rows_dev, cols_dev = amplitudes.shape
    width = rows_dev * TS
    tiles = ZH * ZL
    ids = jnp.arange(tiles, dtype=jnp.int32)

    def entry(i):
        return jnp.sum(jnp.where(ids == i, partner, 0))

    half = entry(z) % 2
    mine = jnp.where(half == 0, amplitudes[:, :, :TS], amplitudes[:, :, TS:]).reshape(pairs, width)
    sent = jnp.broadcast_to(mine[None], (tiles, pairs, width))
    got = lax.all_to_all(sent, ("zh", "zl"), 0, 0, tiled=True)
    chosen = jnp.stack(
        [lax.dynamic_slice(got, (entry(2 * row + h), 0, 0), (1, pairs, width))[0] for h in range(2)]
    )
    sent = jnp.broadcast_to(chosen[None], (X * CORE, 2, pairs, width))
    packed = lax.all_to_all(sent, ("x", "core"), 0, 0, tiled=True)
    group = ZL * ROW
    partials = pl.pallas_call(
        matmul_kernel,
        out_shape=jax.ShapeDtypeStruct((group, pairs, integrals.shape[0]), jnp.float32),
        in_specs=[pl.BlockSpec(memory_space=pltpu.VMEM)] * 2,
        out_specs=pl.BlockSpec(memory_space=pltpu.VMEM),
        compiler_params=pltpu.CompilerParams(vmem_limit_bytes=40 * 1024 * 1024),
        name="ladder_matmul",
    )(packed, integrals)
    shared = lax.all_to_all(partials, ("zl", "row"), 0, 0, tiled=True)
    sums = jnp.sum(shared.reshape(ZL, ROW, pairs, width), axis=1)
    off = jnp.array(REACH, jnp.int32)[(row - zh) % ROW]
    target = jnp.where(zl == 0, 2 * zh - off + tiles, 2 * zh + 1 + off) % tiles
    bra = entry(target)
    block = jnp.where(bra % 2 == 0, sums[0], sums[1]).astype(jnp.bfloat16).reshape(pairs, rows_dev, TS)
    useful = bra // 2 == zh
    zero = jnp.zeros_like(block)
    left = jnp.where(useful & (bra % 2 == 0), block, zero)
    right = jnp.where(useful & (bra % 2 == 1), block, zero)
    out = jnp.concatenate([left, right], axis=2)
    return lax.ppermute(out, AXES, delivery_pairs())


def solution(mesh):
    fine = Mesh(mesh.devices.reshape(ZH, ZL, X, CORE, ROW), AXES)
    col = ("zh", "zl", "x", "core")
    return jax.shard_map(
        per_device,
        mesh=fine,
        in_specs=(P(None, col, "row"), P(col, "row"), P()),
        out_specs=P(None, col, "row"),
        check_vma=False,
    )
```

time: 192 us -> 61.7 us (0.32)
  waiting for transfers between devices: 141 us -> 11.7 us
  starting transfers between devices: 0.04 us -> 16 us
  between operations: 18.2 us -> 9.81 us
  matrix products: 5.65 us -> 0 us
  blocking collectives: 16.1 us -> 11.6 us
  Pallas kernels: 0 us -> 2.98 us
    all_gather x2 -> x0, waiting for transfers between devices: 141 us -> none  [the longest x1 75.3 us: per_device(): gathered = lax.all_gather(amplitudes, 'col', axis=1, tiled=True)]
    psum x1 -> x0, blocking collectives: 16.1 us -> none  [per_device(): finished = lax.psum(partial_sum, 'row').astype(jnp.bfloat16)]
    all_to_all x0 -> x2, starting transfers between devices: none -> 13.3 us  [the longest x1 8.47 us: per_device(): got = lax.all_to_all(sent, ('zh', 'zl'), 0, 0, tiled=True)]
    all_to_all x0 -> x1, blocking collectives: none -> 11.6 us  [per_device(): packed = lax.all_to_all(sent, ('x', 'core'), 0, 0, tiled=True)]
    all_to_all x0 -> x2, waiting for transfers between devices: none -> 7.36 us  [the longest x1 5.37 us: per_device(): got = lax.all_to_all(sent, ('zh', 'zl'), 0, 0, tiled=True)]
    dot_general x1 -> x0, matrix products: 5.65 us -> none  [per_device(): lax.dot_general(packed, integrals, (((1,), (1,)), ((), ())), preferred_el...]
    ppermute x0 -> x1, waiting for transfers between devices: none -> 4.36 us  [per_device(): return lax.ppermute(out, AXES, delivery_pairs())]
    unnamed x2 -> x3, local copies, waits for them, and re-layouts: 0.01 us -> 4 us
  transfers between devices with their start and end apart: 2 -> 3, of which waited for: 2 -> 3; matrix products, arithmetic and copies ran while one was open for 1% -> 0% of each run, Pallas kernels for 0% -> 0%
where the time goes in v1:
time: 61.7 us; the launch traced here: 60.7 us
  starting transfers between devices  16 us (26%)
  waiting for transfers between devices  11.7 us (19%)
  blocking collectives  11.6 us (19%)
  between operations  9.81 us (16%)
  local copies, waits for them, and re-layouts  6.19 us (10%)
  Pallas kernels  2.98 us (5%)
  other arithmetic  2.45 us (4%)
    all_to_all x1, blocking collectives, per_device(): packed = lax.all_to_all(sent, ('x', 'core'), 0, 0, tiled=True)  11.6 us
    all_to_all x1, starting transfers between devices, per_device(): got = lax.all_to_all(sent, ('zh', 'zl'), 0, 0, tiled=True)  8.47 us
    all_to_all x1, waiting for transfers between devices, per_device(): got = lax.all_to_all(sent, ('zh', 'zl'), 0, 0, tiled=True)  5.37 us
    all_to_all x1, starting transfers between devices, per_device(): shared = lax.all_to_all(partials, ('zl', 'row'), 0, 0, tiled=True)  4.8 us
    ppermute x1, waiting for transfers between devices, per_device(): return lax.ppermute(out, AXES, delivery_pairs())  4.36 us
    unnamed x3, local copies, waits for them, and re-layouts  4 us
    pallas_call x1, Pallas kernels, per_device(): pl.pallas_call(matmul_kernel, out_shape=jax.ShapeDtypeStruct((group, pair...  2.98 us
    ppermute x1, starting transfers between devices, per_device(): return lax.ppermute(out, AXES, delivery_pairs())  2.69 us
  transfers between devices with their start and end apart: 3, of which 3 were waited for; matrix products, arithmetic and copies ran while one was open for 0% of the time, Pallas kernels for 0%

profile of v1, /device:TPU:16, one launch (start us, length us, event | category | flops | bytes accessed | tf_op | source)
XLA Modules:
  0.0 60.7 jit_solution(13971133668770769605)
XLA Ops:
  0.0 1.2 %dynamic_slice.9 = s32[1]{0:T(128)} dynamic-slice(s32[4]{0:T(128)} %constant.74.clone, s32[]{:T(128)S(6)} %select_n.89), dynamic_slice_sizes={1} | dynamic-slice | bytes 12 | tf_op jit(solution)/shard_map/dynamic_slice | solution.py:84
  2.6 1.4 %fusion.1 = (s32[]{:T(128)}, s32[]{:T(128)}, s32[]{:T(128)}, s32[]{:T(128)}) fusion(s32[8]{0:T(128)} %param.6, s32[]{:T(128)S(6)} %select_n.91, s32[]{:T(128)S(6)} %add.47, s32[]{:T(128)S(6)} %add.50, s32[]{:T(128)S(6)} %mul.10), kind=kLoop, calls=%fused_computation.12 | loop fusion | flops 92 | bytes 64 | tf_op jit(solution)/shard_map/reduce_sum | solution.py:62
  6.1 0.9 %slice_select_fusion.1 = bf16[16,8,64]{2,1,0:T(8,128)(2,1)S(1)} fusion(bf16[16,8,128]{2,1,0:T(8,128)(2,1)} %param.4, pred[]{:T(512)S(6)} %eq.54), kind=kLoop, calls=%fused_computation.5 | loop fusion | flops 8192 | bytes 49153 | tf_op jit(solution)/shard_map/jit(_where)/select_n | solution.py:65
  7.0 0.1 broadcast_in_dim.24
  7.1 0.6 %broadcast_in_dim.25 = bf16[8,16,512]{2,1,0:T(8,128)(2,1)} broadcast(bf16[16,512]{1,0:T(8,128)(2,1)S(1)} %broadcast_in_dim.24), dimensions={1,2} | broadcast | bytes 147456 | tf_op jit(solution)/shard_map/broadcast_in_dim | solution.py:66
  7.7 8.5 %all-to-all-start = ((bf16[8,16,512]{2,1,0:T(8,128)(2,1)}), bf16[8,16,512]{2,1,0:T(8,128)(2,1)S(1)}, u32[]{:S(2)}, u32[]{:S(2)}) async-start(bf16[8,16,512]{2,1,0:T(8,128)(2,1)} %broadcast_in_dim.25), calls=%async_computation | async-start | bytes 262144 | tf_op jit(solution)/shard_map/all_to_all | solution.py:67
  19.9 5.4 %all-to-all-done = bf16[8,16,512]{2,1,0:T(8,128)(2,1)S(1)} async-done(((bf16[8,16,512]{2,1,0:T(8,128)(2,1)}), bf16[8,16,512]{2,1,0:T(8,128)(2,1)S(1)}, u32[]{:S(2)}, u32[]{:S(2)}) %all-to-all-start) | async-done | bytes 131104 | tf_op jit(solution)/shard_map/all_to_all | solution.py:67
  25.3 11.6 %all_to_all.15.packed_ref = bf16[8,2,16,512]{3,2,1,0:T(8,128)(2,1)S(1)} all-to-all(bf16[8,2,16,512]{3,2,1,0:T(8,128)(2,1)S(1)} %broadcast_in_dim.26), channel_id=1, replica_groups=mesh['zh'=4,'zl'=2,'x'=4,'core'=2,'row'=4] {'x','core'}, dimensions={0} | all-to-all | bytes 524288 | tf_op jit(solution)/shard_map/all_to_all | solution.py:72
  37.0 0.0 copy-start
  37.0 3.4 %copy-done = bf16[512,8192]{1,0:T(8,128)(2,1)S(1)} copy-done((bf16[512,8192]{1,0:T(8,128)(2,1)S(1)}, bf16[512,8192]{1,0:T(8,128)(2,1)}, u32[]{:S(2)}) %copy-start) | copy-done | bytes 8388632
  40.3 3.0 %ladder_matmul.1 = f32[8,16,512]{2,1,0:T(8,128)} custom-call(bf16[8,2,16,512]{3,2,1,0:T(8,128)(2,1)S(1)} %all_to_all.15.packed_ref, bf16[512,8192]{1,0:T(8,128)(2,1)S(1)} %copy-done), custom_call_target="tpu_custom_call" | custom-call | tf_op jit(solution)/shard_map/ladder_matmul/pallas_call | solution.py:74
  43.3 4.8 %all-to-all-start.2 = ((f32[8,16,512]{2,1,0:T(8,128)}), f32[8,16,512]{2,1,0:T(8,128)S(1)}, u32[]{:S(2)}, u32[]{:S(2)}) async-start(f32[8,16,512]{2,1,0:T(8,128)} %ladder_matmul.1), calls=%async_computation.2 | async-start | bytes 524288 | tf_op jit(solution)/shard_map/all_to_all | solution.py:82
  50.8 2.0 %all-to-all-done.2 = f32[8,16,512]{2,1,0:T(8,128)S(1)} async-done(((f32[8,16,512]{2,1,0:T(8,128)}), f32[8,16,512]{2,1,0:T(8,128)S(1)}, u32[]{:S(2)}, u32[]{:S(2)}) %all-to-all-start.2) | async-done | bytes 262176 | tf_op jit(solution)/shard_map/all_to_all | solution.py:82
  52.8 0.1 select_n.110
  52.9 0.1 select_n.107
  53.0 0.1 pad_maximum_fusion.1
  53.1 2.7 %collective-permute-start = (bf16[16,8,128]{2,1,0:T(8,128)(2,1)S(1)}, bf16[16,8,128]{2,1,0:T(8,128)(2,1)S(1)}, u32[]{:S(2)}, u32[]{:S(2)}) collective-permute-start(bf16[16,8,128]{2,1,0:T(8,128)(2,1)S(1)} %pad_maximum_fusion.1), channel_id=1, source_target_pairs={{0,160},{1,224},{2,0},{3,192},{4,164},{5,228},{6,4},{7,196},{8,168... | collective-permute-start | bytes 98312 | tf_op jit(solution)/shard_map/ppermute | solution.py:93
  55.8 4.4 %collective-permute-done = bf16[16,8,128]{2,1,0:T(8,128)(2,1)S(1)} collective-permute-done((bf16[16,8,128]{2,1,0:T(8,128)(2,1)S(1)}, bf16[16,8,128]{2,1,0:T(8,128)(2,1)S(1)}, u32[]{:S(2)}, u32[]{:S(2)}) %collective-permute-start) | collective-permute-done | bytes 32800 | tf_op jit(solution)/shard_map/ppermute | solution.py:93
  60.1 0.6 %copy.6 = bf16[16,8,128]{2,1,0:T(8,128)(2,1)} copy(bf16[16,8,128]{2,1,0:T(8,128)(2,1)S(1)} %collective-permute-done) | data formatting | bytes 65536
  (6 shorter events, 0.1 us)
Async XLA Ops:
  7.7 17.6 %all-to-all-start = ((bf16[8,16,512]{2,1,0:T(8,128)(2,1)}), bf16[8,16,512]{2,1,0:T(8,128)(2,1)S(1)}, u32[]{:S(2)}, u32[]{:S(2)}) async-start(bf16[8,16,512]{2,1,0:T(8,128)(2,1)} %broadcast_in_dim.25), calls=%async_computation | async-start | bytes 262144 | tf_op jit(solution)/shard_map/all_to_all | solution.py:67
  37.0 3.4 %copy-start = (bf16[512,8192]{1,0:T(8,128)(2,1)S(1)}, bf16[512,8192]{1,0:T(8,128)(2,1)}, u32[]{:S(2)}) copy-start(bf16[512,8192]{1,0:T(8,128)(2,1)} %integrals_ref.1) | copy-start | bytes 25165828
  43.3 9.4 %all-to-all-start.2 = ((f32[8,16,512]{2,1,0:T(8,128)}), f32[8,16,512]{2,1,0:T(8,128)S(1)}, u32[]{:S(2)}, u32[]{:S(2)}) async-start(f32[8,16,512]{2,1,0:T(8,128)} %ladder_matmul.1), calls=%async_computation.2 | async-start | bytes 524288 | tf_op jit(solution)/shard_map/all_to_all | solution.py:82
  53.1 7.1 %collective-permute-start = (bf16[16,8,128]{2,1,0:T(8,128)(2,1)S(1)}, bf16[16,8,128]{2,1,0:T(8,128)(2,1)S(1)}, u32[]{:S(2)}, u32[]{:S(2)}) collective-permute-start(bf16[16,8,128]{2,1,0:T(8,128)(2,1)S(1)} %pad_maximum_fusion.1), channel_id=1, source_target_pairs={{0,160},{1,224},{2,0},{3,192},{4,164},{5,228},{6,4},{7,196},{8,168... | collective-permute-start | bytes 98312 | tf_op jit(solution)/shard_map/ppermute | solution.py:93

commit v2 on v1

v2 whole, which is shorter than its diff:
```python
import jax
import jax.numpy as jnp
from jax import lax
from jax.experimental import pallas as pl
from jax.experimental.pallas import tpu as pltpu
from jax.sharding import Mesh
from jax.sharding import PartitionSpec as P

TS = 64
ZH, ZL, X, CORE, ROW = 4, 2, 4, 2, 4
TILES = ZH * ZL
AXES = ("zh", "zl", "x", "core", "row")
PIECES = 8
REACH = (3, 1, 0, 2)
VMEM = pl.BlockSpec(memory_space=pltpu.VMEM)
HBM = pl.BlockSpec(memory_space=pltpu.HBM)


def target_z(zh, zl, row):
    off = REACH[(row - zh) % ROW]
    return (2 * zh - off) % TILES if zl == 0 else (2 * zh + 1 + off) % TILES


def linear(zh, zl, x, core, row):
    return (((zh * ZL + zl) * X + x) * CORE + core) * ROW + row


def delivery_pairs():
    pairs = []
    for zh in range(ZH):
        for zl in range(ZL):
            for x in range(X):
                for core in range(CORE):
                    for row in range(ROW):
                        t = target_z(zh, zl, row)
                        pairs.append((linear(zh, zl, x, core, row), linear(t // ZL, t % ZL, x, core, zh)))
    return pairs


def in_vmem(x):
    return pltpu.with_memory_space_constraint(x, pltpu.VMEM)


def in_hbm(x):
    return pltpu.with_memory_space_constraint(x, pltpu.HBM)


def lower_lanes(rows):
    return lax.broadcasted_iota(jnp.int32, (rows, 2 * TS), 1) < TS


def fetch(copies):
    for copy in copies:
        copy.start()
    for copy in copies:
        copy.wait()


def prepare_kernel(partner_hbm, amplitudes_hbm, sent_ref, pick_ref, keep_ref, partner_ref, amplitudes_ref, sems):
    fetch(
        [
            pltpu.make_async_copy(partner_hbm, partner_ref, sems.at[0]),
            pltpu.make_async_copy(amplitudes_hbm, amplitudes_ref, sems.at[1]),
        ]
    )
    zh, zl, row = lax.axis_index("zh"), lax.axis_index("zl"), lax.axis_index("row")
    for h in range(2):
        source = partner_ref[2 * row + h]
        for z in range(TILES):
            pick_ref[h, z] = jnp.full(pick_ref.shape[2:], jnp.where(source == z, 1, 0), jnp.int32)
    turn = (row - zh + ROW) % ROW
    off = jnp.where(turn == 0, REACH[0], jnp.where(turn == 1, REACH[1], jnp.where(turn == 2, REACH[2], REACH[3])))
    target = jnp.where(zl == 0, 2 * zh - off + TILES, 2 * zh + 1 + off) % TILES
    bra = partner_ref[target]
    for h in range(2):
        keep_ref[h] = jnp.full(keep_ref.shape[1:], jnp.where(bra == 2 * zh + h, 1, 0), jnp.int32)
    z = zh * ZL + zl
    upper = partner_ref[z] % 2 == 1
    rows = jnp.swapaxes(amplitudes_ref[...].astype(jnp.float32), 0, 1)
    units, pairs, _ = rows.shape
    lower = lower_lanes(pairs)
    columns = []
    for j in range(units // 2):
        first, second = rows[2 * j], rows[2 * j + 1]
        from_lower = jnp.where(lower, first, pltpu.roll(second, TS, 1))
        from_upper = jnp.where(lower, pltpu.roll(first, TS, 1), second)
        columns.append(jnp.where(upper, from_upper, from_lower))
    mine = jnp.concatenate(columns, axis=1).astype(sent_ref.dtype)
    for j in range(sent_ref.shape[0]):
        sent_ref[j] = mine


def choose_kernel(pick_ref, got_ref, chosen_ref):
    tiles, pairs, width = got_ref.shape
    reps = width // pick_ref.shape[3]
    for h in range(2):
        chosen = jnp.zeros((pairs, width), jnp.float32)
        for z in range(tiles):
            wanted = jnp.concatenate([pick_ref[h, z]] * reps, axis=1) != 0
            chosen = jnp.where(wanted, got_ref[z].astype(jnp.float32), chosen)
        chosen_ref[h] = chosen.astype(chosen_ref.dtype)


def stage_kernel(integrals_ref, staged_ref, sems):
    step = integrals_ref.shape[0] // PIECES
    parts = [pl.ds(j * step, step) for j in range(PIECES)]
    fetch([pltpu.make_async_copy(integrals_ref.at[p, :], staged_ref.at[p, :], sems.at[j]) for j, p in enumerate(parts)])


def product(packed_ref, integrals_ref, core, places):
    width = packed_ref.shape[3]
    total = jnp.zeros((packed_ref.shape[2], integrals_ref.shape[0]), jnp.float32)
    for i, x in enumerate(places):
        for h in range(2):
            start = pl.multiple_of(((h * X + x) * CORE + core) * width, width)
            total = total + lax.dot_general(
                packed_ref[i, h],
                integrals_ref[:, pl.ds(start, width)],
                (((1,), (1,)), ((), ())),
                preferred_element_type=jnp.float32,
            )
    return total


def join_kernel(first_ref, second_ref, *rest):
    out_ref = rest[-1]
    count = first_ref.shape[0]
    out_ref[pl.ds(0, count)] = first_ref[...]
    out_ref[pl.ds(count, count)] = second_ref[...]


def near(x):
    return x + 1 - 2 * (x % 2)


def near_kernel(packed_ref, integrals_ref, out_ref):
    x = lax.axis_index("x")
    out_ref[...] = product(packed_ref, integrals_ref, lax.axis_index("core"), [x, near(x)])


def far_kernel(packed_ref, before_ref, integrals_ref, out_ref):
    x = X - 1 - lax.axis_index("x")
    out_ref[...] = before_ref[...] + product(packed_ref, integrals_ref, lax.axis_index("core"), [x, near(x)])


def other_kernel(packed_ref, before_ref, integrals_ref, out_ref):
    x = lax.axis_index("x")
    y = X - 1 - x
    places = [x, near(x), y, near(y)]
    total = before_ref[...] + product(packed_ref, integrals_ref, 1 - lax.axis_index("core"), places)
    for j in range(out_ref.shape[0]):
        out_ref[j] = total


def finish_kernel(keep_ref, shared_ref, out_ref):
    pairs, width = shared_ref.shape[1:]
    sums = []
    for h in range(2):
        total = shared_ref[h * ROW]
        for j in range(1, ROW):
            total = total + shared_ref[h * ROW + j]
        wanted = jnp.concatenate([keep_ref[h]] * (width // keep_ref.shape[2]), axis=1) != 0
        total = jnp.where(wanted, total, 0.0)
        sums.append(total.astype(jnp.bfloat16).astype(jnp.float32))
    lower = lower_lanes(pairs)
    rows = []
    for j in range(width // (2 * TS)):
        part = slice(j * 2 * TS, (j + 1) * 2 * TS)
        left, right = sums[0][:, part], sums[1][:, part]
        rows.append(jnp.where(lower, left, pltpu.roll(right, TS, 1)))
        rows.append(jnp.where(lower, pltpu.roll(left, TS, 1), right))
    out_ref[...] = jnp.swapaxes(jnp.stack(rows, 0), 0, 1).astype(out_ref.dtype)


def per_device(amplitudes, integrals, partner):
    pairs, rows_dev, _ = amplitudes.shape
    width = rows_dev * TS
    bra = integrals.shape[0]
    params = pltpu.CompilerParams(vmem_limit_bytes=4 * 1024 * 1024)
    sent, pick, keep = pl.pallas_call(
        prepare_kernel,
        out_shape=[
            pltpu.VMEM((TILES, pairs, width), jnp.bfloat16),
            pltpu.VMEM((2, TILES, pairs, 128), jnp.int32),
            pltpu.VMEM((2, pairs, 128), jnp.int32),
        ],
        in_specs=[HBM, HBM],
        out_specs=[VMEM, VMEM, VMEM],
        scratch_shapes=[
            pltpu.SMEM(partner.shape, partner.dtype),
            pltpu.VMEM(amplitudes.shape, amplitudes.dtype),
            pltpu.SemaphoreType.DMA((2,)),
        ],
        compiler_params=params,
        name="prepare",
    )(in_hbm(partner), in_hbm(amplitudes))
    got = lax.all_to_all(sent, ("zh", "zl"), 0, 0, tiled=True)
    chosen = pl.pallas_call(
        choose_kernel,
        out_shape=pltpu.VMEM((2, pairs, width), jnp.bfloat16),
        in_specs=[VMEM, VMEM],
        out_specs=VMEM,
        compiler_params=params,
        name="choose",
    )(in_vmem(pick), in_vmem(got))
    staged = pl.pallas_call(
        stage_kernel,
        out_shape=pltpu.VMEM(integrals.shape, integrals.dtype),
        in_specs=[HBM],
        out_specs=VMEM,
        scratch_shapes=[pltpu.SemaphoreType.DMA((PIECES,))],
        compiler_params=params,
        cost_estimate=pl.CostEstimate(flops=0, bytes_accessed=2 * integrals.size, transcendentals=0),
        name="stage",
    )(in_hbm(integrals))

    def multiply(kernel, operands, share, copies, name):
        shape = (pairs, bra) if copies == 1 else (copies, pairs, bra)
        operands = [*operands, staged]
        return pl.pallas_call(
            kernel,
            out_shape=pltpu.VMEM(shape, jnp.float32),
            in_specs=[VMEM] * len(operands),
            out_specs=VMEM,
            compiler_params=params,
            cost_estimate=pl.CostEstimate(
                flops=2 * pairs * integrals.size // share,
                bytes_accessed=2 * integrals.size // share,
                transcendentals=0,
            ),
            name=name,
        )(*[in_vmem(operand) for operand in operands])

    def join(operands):
        first = operands[0]
        return pl.pallas_call(
            join_kernel,
            out_shape=pltpu.VMEM((2 * first.shape[0], *first.shape[1:]), first.dtype),
            in_specs=[VMEM, VMEM, VMEM],
            out_specs=VMEM,
            compiler_params=params,
            name="join",
        )(*[in_vmem(operand) for operand in operands])

    beside = lax.ppermute(chosen, "x", [(i, i ^ 1) for i in range(X)])
    couple = join([chosen[None], beside[None], staged])
    across = lax.ppermute(couple, "x", [(i, X - 1 - i) for i in range(X)])
    total = multiply(near_kernel, [couple], 4, 1, "near_product")
    four = join([couple, across, total])
    neighbour = lax.ppermute(four, "core", [(0, 1), (1, 0)])
    total = multiply(far_kernel, [across, total], 4, 1, "far_product")
    partials = multiply(other_kernel, [neighbour, total], 2, ZL * ROW, "other_product")
    shared = lax.all_to_all(partials, ("zl", "row"), 0, 0, tiled=True)
    out = pl.pallas_call(
        finish_kernel,
        out_shape=pltpu.VMEM(amplitudes.shape, jnp.bfloat16),
        in_specs=[VMEM, VMEM],
        out_specs=VMEM,
        compiler_params=params,
        name="finish",
    )(in_vmem(keep), in_vmem(shared))
    return lax.ppermute(out, AXES, delivery_pairs())


def solution(mesh):
    fine = Mesh(mesh.devices.reshape(ZH, ZL, X, CORE, ROW), AXES)
    col = ("zh", "zl", "x", "core")
    return jax.shard_map(
        per_device,
        mesh=fine,
        in_specs=(P(None, col, "row"), P(col, "row"), P()),
        out_specs=P(None, col, "row"),
        check_vma=False,
    )
```

time: 61.7 us -> 49.4 us (0.80)
  blocking collectives: 11.6 us -> 26.9 us
  between operations: 9.81 us -> 0.06 us
  starting transfers between devices: 16 us -> 6.55 us
  local copies, waits for them, and re-layouts: 6.19 us -> 0.61 us
  Pallas kernels: 2.98 us -> 7.01 us
  waiting for transfers between devices: 11.7 us -> 7.78 us
  other arithmetic: 2.45 us -> 0 us
    all_to_all x1 -> x2, blocking collectives: 11.6 us -> 26.9 us  [the longest x1 17.4 us: per_device(): got = lax.all_to_all(sent, ('zh', 'zl'), 0, 0, tiled=True)]
    all_to_all x2 -> x0, starting transfers between devices: 13.3 us -> none  [the longest x1 8.47 us: per_device(): got = lax.all_to_all(sent, ('zh', 'zl'), 0, 0, tiled=True)]
    all_to_all x2 -> x0, waiting for transfers between devices: 7.36 us -> none  [the longest x1 5.37 us: per_device(): got = lax.all_to_all(sent, ('zh', 'zl'), 0, 0, tiled=True)]
    pallas_call x1 -> x9, Pallas kernels: 2.98 us -> 7.01 us  [the longest x1 3.47 us: per_device(): pl.pallas_call(stage_kernel, out_shape=pltpu.VMEM(integrals.shape, integr...]
    ppermute x0 -> x3, starting transfers between devices: none -> 3.85 us  [the longest x1 2.18 us: per_device(): across = lax.ppermute(couple, 'x', [(i, X - 1 - i) for i in range(X)])]
    ppermute x0 -> x3, waiting for transfers between devices: none -> 3.42 us  [the longest x1 2.74 us: per_device(): across = lax.ppermute(couple, 'x', [(i, X - 1 - i) for i in range(X)])]
    unnamed x3 -> x1, local copies, waits for them, and re-layouts: 4 us -> 0.61 us
    reduce_sum x2 -> x0, other arithmetic: 1.42 us -> none  [the longest x1 1.4 us: entry(): return jnp.sum(jnp.where(ids == i, partner, 0))]
  transfers between devices with their start and end apart: 3 -> 4, of which waited for: 3 -> 3; matrix products, arithmetic and copies ran while one was open for 0% -> 0% of each run, Pallas kernels for 0% -> 10%
where the time goes in v2:
time: 49.4 us; the launch traced here: 48.9 us
  blocking collectives  26.9 us (54%)
  waiting for transfers between devices  7.78 us (16%)
  Pallas kernels  7.01 us (14%)
  starting transfers between devices  6.55 us (13%)
  local copies, waits for them, and re-layouts  0.61 us (1%)
    all_to_all x1, blocking collectives, per_device(): got = lax.all_to_all(sent, ('zh', 'zl'), 0, 0, tiled=True)  17.4 us
    all_to_all x1, blocking collectives, per_device(): shared = lax.all_to_all(partials, ('zl', 'row'), 0, 0, tiled=True)  9.52 us
    ppermute x1, waiting for transfers between devices, per_device(): return lax.ppermute(out, AXES, delivery_pairs())  4.36 us
    pallas_call x1, Pallas kernels, per_device(): pl.pallas_call(stage_kernel, out_shape=pltpu.VMEM(integrals.shape, integr...  3.47 us
    ppermute x1, waiting for transfers between devices, per_device(): across = lax.ppermute(couple, 'x', [(i, X - 1 - i) for i in range(X)])  2.74 us
    ppermute x1, starting transfers between devices, per_device(): return lax.ppermute(out, AXES, delivery_pairs())  2.69 us
    pallas_call x3, Pallas kernels, multiply(): pl.pallas_call(kernel, out_shape=pltpu.VMEM(shape, jnp.float32), in_specs...  2.51 us
    ppermute x1, starting transfers between devices, per_device(): across = lax.ppermute(couple, 'x', [(i, X - 1 - i) for i in range(X)])  2.18 us
  transfers between devices with their start and end apart: 4, of which 3 were waited for; matrix products, arithmetic and copies ran while one was open for 0% of the time, Pallas kernels for 10%

profile of v2, /device:TPU:16, one launch (start us, length us, event | category | flops | bytes accessed | tf_op | source)
XLA Modules:
  0.0 48.9 jit_solution(543532860496395668)
XLA Ops:
  0.0 0.9 %prepare.1 = (bf16[8,16,512]{2,1,0:T(8,128)(2,1)S(1)}, s32[2,8,16,128]{3,2,1,0:T(8,128)S(1)}, s32[2,16,128]{2,1,0:T(8,128)S(1)}) custom-call(s32[8]{0:T(128)} %partner_hbm.1, bf16[16,8,128]{2,1,0:T(8,128)(2,1)} %amplitudes_hbm.1), custom_call_target="tpu_custom_call" | custom-call | tf_op jit(solution)/shard_map/prepare/pallas_call | solution.py:180
  0.9 17.4 %all_to_all.10.got_ref = bf16[8,16,512]{2,1,0:T(8,128)(2,1)S(1)} all-to-all(bf16[8,16,512]{2,1,0:T(8,128)(2,1)S(1)} %get-tuple-element.10), channel_id=1, replica_groups=mesh['zh'=4,'zl'=2,'x'=4,'core'=2,'row'=4] {'zh','zl'}, dimensions={0} | all-to-all | bytes 262144 | tf_op jit(solution)/shard_map/all_to_all | solution.py:197
  18.3 1.6 %collective-permute-start = (bf16[2,16,512]{2,1,0:T(8,128)(2,1)S(1)}, bf16[2,16,512]{2,1,0:T(8,128)(2,1)S(1)}, u32[]{:S(2)}, u32[]{:S(2)}) collective-permute-start(bf16[2,16,512]{2,1,0:T(8,128)(2,1)S(1)} %choose.1), channel_id=1, source_target_pairs={{0,8},{8,0},{16,24},{24,16},{1,9},{9,1},{17,25},{25,17},{2,10},{10... | collective-permute-start | bytes 98312 | tf_op jit(solution)/shard_map/ppermute | solution.py:245
  19.9 3.5 %stage.1.rest_0_.integrals_ref = bf16[512,8192]{1,0:T(8,128)(2,1)S(1)} custom-call(bf16[512,8192]{1,0:T(8,128)(2,1)} %integrals_ref.1), custom_call_target="tpu_custom_call" | custom-call | bytes 8388608 | tf_op jit(solution)/shard_map/stage/pallas_call | solution.py:206
  23.3 0.0 collective-permute-done
  23.4 2.2 %collective-permute-start.1 = (bf16[2,2,16,512]{3,2,1,0:T(8,128)(2,1)S(1)}, bf16[2,2,16,512]{3,2,1,0:T(8,128)(2,1)S(1)}, u32[]{:S(2)}, u32[]{:S(2)}) collective-permute-start(bf16[2,2,16,512]{3,2,1,0:T(8,128)(2,1)S(1)} %join.2.packed_ref.first_ref), channel_id=1, source_target_pairs={{0,24},{8,16},{16,8},{24,0},{1,25},{9,17},{17,9},{25,1},{2,26},{10... | collective-permute-start | bytes 196616 | tf_op jit(solution)/shard_map/ppermute | solution.py:247
  25.5 0.6 %near_product.1.rest_0_.before_ref = f32[16,512]{1,0:T(8,128)S(1)} custom-call(bf16[2,2,16,512]{3,2,1,0:T(8,128)(2,1)S(1)} %join.2.packed_ref.first_ref, bf16[512,8192]{1,0:T(8,128)(2,1)S(1)} %stage.1.rest_0_.integrals_ref), custom_call_target="tpu_custom_call" | custom-call | flops 33554432 | bytes 2097152 | tf_op jit(solution)/shard_map/near_product/pallas_call | solution.py:220
  26.2 2.7 %collective-permute-done.1.second_ref.packed_ref = bf16[2,2,16,512]{3,2,1,0:T(8,128)(2,1)S(1)} collective-permute-done((bf16[2,2,16,512]{3,2,1,0:T(8,128)(2,1)S(1)}, bf16[2,2,16,512]{3,2,1,0:T(8,128)(2,1)S(1)}, u32[]{:S(2)}, u32[]{:S(2)}) %collective-permute-start.1) | collective-permute-done | bytes 65568 | tf_op jit(solution)/shard_map/ppermute | solution.py:247
  28.9 0.1 collective-permute-start.2
  29.0 0.7 %far_product.1.before_ref = f32[16,512]{1,0:T(8,128)S(1)} custom-call(bf16[2,2,16,512]{3,2,1,0:T(8,128)(2,1)S(1)} %collective-permute-done.1.second_ref.packed_ref, f32[16,512]{1,0:T(8,128)S(1)} %near_product.1.rest_0_.before_ref, bf16[512,8192]{1,0:T(8,128)(2,1)S(1)} %stage.1.rest_0_.integrals_ref), custom_call_target="tpu_custom_call" | custom-call | flops 33554432 | bytes 2097152 | tf_op jit(solution)/shard_map/far_product/pallas_call | solution.py:220
  29.7 0.7 %collective-permute-done.2.packed_ref = bf16[4,2,16,512]{3,2,1,0:T(8,128)(2,1)S(1)} collective-permute-done((bf16[4,2,16,512]{3,2,1,0:T(8,128)(2,1)S(1)}, bf16[4,2,16,512]{3,2,1,0:T(8,128)(2,1)S(1)}, u32[]{:S(2)}, u32[]{:S(2)}) %collective-permute-start.2) | collective-permute-done | bytes 131104 | tf_op jit(solution)/shard_map/ppermute | solution.py:250
  30.4 1.2 %other_product.1 = f32[8,16,512]{2,1,0:T(8,128)S(1)} custom-call(bf16[4,2,16,512]{3,2,1,0:T(8,128)(2,1)S(1)} %collective-permute-done.2.packed_ref, f32[16,512]{1,0:T(8,128)S(1)} %far_product.1.before_ref, bf16[512,8192]{1,0:T(8,128)(2,1)S(1)} %stage.1.rest_0_.integrals_ref), custom_call_target="tpu_custom_call" | custom-call | flops 67108864 | bytes 4194304 | tf_op jit(solution)/shard_map/other_product/pallas_call | solution.py:220
  31.6 9.5 %all_to_all.11.shared_ref = f32[8,16,512]{2,1,0:T(8,128)S(1)} all-to-all(f32[8,16,512]{2,1,0:T(8,128)S(1)} %other_product.1), channel_id=1, replica_groups=mesh['zh'=4,'zl'=2,'x'=4,'core'=2,'row'=4] {'zl','row'}, dimensions={0} | all-to-all | bytes 524288 | tf_op jit(solution)/shard_map/all_to_all | solution.py:253
  41.1 0.1 finish.1
  41.2 2.7 %collective-permute-start.3 = (bf16[16,8,128]{2,1,0:T(8,128)(2,1)S(1)}, bf16[16,8,128]{2,1,0:T(8,128)(2,1)S(1)}, u32[]{:S(2)}, u32[]{:S(2)}) collective-permute-start(bf16[16,8,128]{2,1,0:T(8,128)(2,1)S(1)} %finish.1), channel_id=1, source_target_pairs={{0,160},{1,224},{2,0},{3,192},{4,164},{5,228},{6,4},{7,196},{8,168... | collective-permute-start | bytes 98312 | tf_op jit(solution)/shard_map/ppermute | solution.py:262
  43.9 4.4 %collective-permute-done.3 = bf16[16,8,128]{2,1,0:T(8,128)(2,1)S(1)} collective-permute-done((bf16[16,8,128]{2,1,0:T(8,128)(2,1)S(1)}, bf16[16,8,128]{2,1,0:T(8,128)(2,1)S(1)}, u32[]{:S(2)}, u32[]{:S(2)}) %collective-permute-start.3) | collective-permute-done | bytes 32800 | tf_op jit(solution)/shard_map/ppermute | solution.py:262
  48.3 0.6 %copy.5 = bf16[16,8,128]{2,1,0:T(8,128)(2,1)} copy(bf16[16,8,128]{2,1,0:T(8,128)(2,1)S(1)} %collective-permute-done.3) | data formatting | bytes 65536
  (3 shorter events, 0.1 us)
Async XLA Ops:
  18.3 5.1 %collective-permute-start = (bf16[2,16,512]{2,1,0:T(8,128)(2,1)S(1)}, bf16[2,16,512]{2,1,0:T(8,128)(2,1)S(1)}, u32[]{:S(2)}, u32[]{:S(2)}) collective-permute-start(bf16[2,16,512]{2,1,0:T(8,128)(2,1)S(1)} %choose.1), channel_id=1, source_target_pairs={{0,8},{8,0},{16,24},{24,16},{1,9},{9,1},{17,25},{25,17},{2,10},{10... | collective-permute-start | bytes 98312 | tf_op jit(solution)/shard_map/ppermute | solution.py:245
  23.4 5.6 %collective-permute-start.1 = (bf16[2,2,16,512]{3,2,1,0:T(8,128)(2,1)S(1)}, bf16[2,2,16,512]{3,2,1,0:T(8,128)(2,1)S(1)}, u32[]{:S(2)}, u32[]{:S(2)}) collective-permute-start(bf16[2,2,16,512]{3,2,1,0:T(8,128)(2,1)S(1)} %join.2.packed_ref.first_ref), channel_id=1, source_target_pairs={{0,24},{8,16},{16,8},{24,0},{1,25},{9,17},{17,9},{25,1},{2,26},{10... | collective-permute-start | bytes 196616 | tf_op jit(solution)/shard_map/ppermute | solution.py:247
  28.9 1.4 %collective-permute-start.2 = (bf16[4,2,16,512]{3,2,1,0:T(8,128)(2,1)S(1)}, bf16[4,2,16,512]{3,2,1,0:T(8,128)(2,1)S(1)}, u32[]{:S(2)}, u32[]{:S(2)}) collective-permute-start(bf16[4,2,16,512]{3,2,1,0:T(8,128)(2,1)S(1)} %join.3), channel_id=1, source_target_pairs={{0,4},{4,0},{1,5},{5,1},{2,6},{6,2},{3,7},{7,3},{8,12},{12,8},{9,1... | collective-permute-start | bytes 393224 | tf_op jit(solution)/shard_map/ppermute | solution.py:250
  41.2 7.1 %collective-permute-start.3 = (bf16[16,8,128]{2,1,0:T(8,128)(2,1)S(1)}, bf16[16,8,128]{2,1,0:T(8,128)(2,1)S(1)}, u32[]{:S(2)}, u32[]{:S(2)}) collective-permute-start(bf16[16,8,128]{2,1,0:T(8,128)(2,1)S(1)} %finish.1), channel_id=1, source_target_pairs={{0,160},{1,224},{2,0},{3,192},{4,164},{5,228},{6,4},{7,196},{8,168... | collective-permute-start | bytes 98312 | tf_op jit(solution)/shard_map/ppermute | solution.py:262

commit v3 on v2

--- a/solution.py
+++ b/solution.py
@@ -101,18 +101,30 @@
         chosen_ref[h] = chosen.astype(chosen_ref.dtype)
 
 
-def stage_kernel(integrals_ref, staged_ref, sems):
-    step = integrals_ref.shape[0] // PIECES
+def stage_top_kernel(integrals_ref, staged_ref, sems):
+    step = staged_ref.shape[0] // PIECES
     parts = [pl.ds(j * step, step) for j in range(PIECES)]
     fetch([pltpu.make_async_copy(integrals_ref.at[p, :], staged_ref.at[p, :], sems.at[j]) for j, p in enumerate(parts)])
 
 
-def product(packed_ref, integrals_ref, core, places):
+def join_kernel(first_ref, second_ref, *rest):
+    out_ref = rest[-1]
+    count = first_ref.shape[0]
+    out_ref[pl.ds(0, count)] = first_ref[...]
+    out_ref[pl.ds(count, count)] = second_ref[...]
+
+
+def after_kernel(value_ref, first_ref, out_ref):
+    out_ref[...] = value_ref[...]
+
+
+def partial_product(packed_ref, integrals_ref, core, x):
     width = packed_ref.shape[3]
+    places = [x, x + 1 - 2 * (x % 2)]
     total = jnp.zeros((packed_ref.shape[2], integrals_ref.shape[0]), jnp.float32)
-    for i, x in enumerate(places):
+    for i, place in enumerate(places):
         for h in range(2):
-            start = pl.multiple_of(((h * X + x) * CORE + core) * width, width)
+            start = pl.multiple_of(((h * X + place) * CORE + core) * width, width)
             total = total + lax.dot_general(
                 packed_ref[i, h],
                 integrals_ref[:, pl.ds(start, width)],
@@ -122,32 +134,50 @@
     return total
 
 
-def join_kernel(first_ref, second_ref, *rest):
-    out_ref = rest[-1]
-    count = first_ref.shape[0]
-    out_ref[pl.ds(0, count)] = first_ref[...]
-    out_ref[pl.ds(count, count)] = second_ref[...]
-
-
-def near(x):
-    return x + 1 - 2 * (x % 2)
-
-
-def near_kernel(packed_ref, integrals_ref, out_ref):
-    x = lax.axis_index("x")
-    out_ref[...] = product(packed_ref, integrals_ref, lax.axis_index("core"), [x, near(x)])
-
-
-def far_kernel(packed_ref, before_ref, integrals_ref, out_ref):
-    x = X - 1 - lax.axis_index("x")
-    out_ref[...] = before_ref[...] + product(packed_ref, integrals_ref, lax.axis_index("core"), [x, near(x)])
-
-
-def other_kernel(packed_ref, before_ref, integrals_ref, out_ref):
-    x = lax.axis_index("x")
-    y = X - 1 - x
-    places = [x, near(x), y, near(y)]
-    total = before_ref[...] + product(packed_ref, integrals_ref, 1 - lax.axis_index("core"), places)
+def product(packed_ref, top_ref, bottom_ref, core, x):
+    return jnp.concatenate([partial_product(packed_ref, ref, core, x) for ref in (top_ref, bottom_ref)], axis=1)
+
+
+def near_kernel(packed_ref, swapped_ref, top_ref, integrals_ref, bottom_ref, out_ref, sems):
+    core, x = lax.axis_index("core"), lax.axis_index("x")
+    rows, columns = bottom_ref.shape
+    span = columns // 4
+    copies = []
+    for n in range(2):
+        pair = (x // 2 + n) % 2
+        for h in range(2):
+            part = pl.ds(pl.multiple_of((2 * h + pair) * span, span), span)
+            source = integrals_ref.at[pl.ds(rows, rows), part]
+            copy = pltpu.make_async_copy(source, bottom_ref.at[:, part], sems.at[len(copies)])
+            copy.start()
+            copies.append(copy)
+
+    def both(ref):
+        return partial_product(packed_ref, ref, core, x) + partial_product(swapped_ref, ref, 1 - core, x)
+
+    @pl.when(core >= 0)
+    def _():
+        out_ref[:, pl.ds(0, rows)] = both(top_ref)
+
+    for copy in copies[:2]:
+        copy.wait()
+
+    @pl.when(x >= 0)
+    def _():
+        out_ref[:, pl.ds(rows, rows)] = both(bottom_ref)
+
+    for copy in copies[2:]:
+        copy.wait()
+
+
+def far_kernel(packed_ref, before_ref, top_ref, bottom_ref, out_ref):
+    core, x = lax.axis_index("core"), X - 1 - lax.axis_index("x")
+    out_ref[...] = before_ref[...] + product(packed_ref, top_ref, bottom_ref, core, x)
+
+
+def last_kernel(packed_ref, before_ref, top_ref, bottom_ref, out_ref):
+    core, x = 1 - lax.axis_index("core"), X - 1 - lax.axis_index("x")
+    total = before_ref[...] + product(packed_ref, top_ref, bottom_ref, core, x)
     for j in range(out_ref.shape[0]):
         out_ref[j] = total
 
@@ -203,53 +233,64 @@
         compiler_params=params,
         name="choose",
     )(in_vmem(pick), in_vmem(got))
-    staged = pl.pallas_call(
-        stage_kernel,
-        out_shape=pltpu.VMEM(integrals.shape, integrals.dtype),
+    staged = pltpu.VMEM((bra // 2, integrals.shape[1]), integrals.dtype)
+
+    def local(kernel, shape, dtype, operands, cost=None, name=None, scratch=(), specs=None):
+        return pl.pallas_call(
+            kernel,
+            out_shape=pltpu.VMEM(shape, dtype),
+            in_specs=specs or [VMEM] * len(operands),
+            out_specs=VMEM,
+            scratch_shapes=scratch,
+            compiler_params=params,
+            cost_estimate=cost,
+            name=name,
+        )(*operands)
+
+    def multiply(kernel, operands, name, copies=()):
+        cost = pl.CostEstimate(
+            flops=pairs * integrals.size // 2, bytes_accessed=integrals.size // 2, transcendentals=0
+        )
+        operands = [in_vmem(operand) for operand in operands]
+        return local(kernel, (*copies, pairs, bra), jnp.float32, operands, cost, name)
+
+    core_swap = [(0, 1), (1, 0)]
+    beside = lax.ppermute(chosen, "x", [(i, i ^ 1) for i in range(X)])
+    top = pl.pallas_call(
+        stage_top_kernel,
+        out_shape=staged,
         in_specs=[HBM],
         out_specs=VMEM,
         scratch_shapes=[pltpu.SemaphoreType.DMA((PIECES,))],
         compiler_params=params,
         cost_estimate=pl.CostEstimate(flops=0, bytes_accessed=2 * integrals.size, transcendentals=0),
-        name="stage",
+        name="stage_top",
     )(in_hbm(integrals))
-
-    def multiply(kernel, operands, share, copies, name):
-        shape = (pairs, bra) if copies == 1 else (copies, pairs, bra)
-        operands = [*operands, staged]
-        return pl.pallas_call(
-            kernel,
-            out_shape=pltpu.VMEM(shape, jnp.float32),
-            in_specs=[VMEM] * len(operands),
-            out_specs=VMEM,
-            compiler_params=params,
-            cost_estimate=pl.CostEstimate(
-                flops=2 * pairs * integrals.size // share,
-                bytes_accessed=2 * integrals.size // share,
-                transcendentals=0,
-            ),
-            name=name,
-        )(*[in_vmem(operand) for operand in operands])
-
-    def join(operands):
-        first = operands[0]
-        return pl.pallas_call(
-            join_kernel,
-            out_shape=pltpu.VMEM((2 * first.shape[0], *first.shape[1:]), first.dtype),
-            in_specs=[VMEM, VMEM, VMEM],
-            out_specs=VMEM,
-            compiler_params=params,
-            name="join",
-        )(*[in_vmem(operand) for operand in operands])
-
-    beside = lax.ppermute(chosen, "x", [(i, i ^ 1) for i in range(X)])
-    couple = join([chosen[None], beside[None], staged])
+    couple = local(
+        join_kernel,
+        (2, 2, pairs, width),
+        chosen.dtype,
+        [in_vmem(chosen[None]), in_vmem(beside[None]), in_vmem(top)],
+        name="join",
+    )
+    swapped = lax.ppermute(couple, "core", core_swap)
     across = lax.ppermute(couple, "x", [(i, X - 1 - i) for i in range(X)])
-    total = multiply(near_kernel, [couple], 4, 1, "near_product")
-    four = join([couple, across, total])
-    neighbour = lax.ppermute(four, "core", [(0, 1), (1, 0)])
-    total = multiply(far_kernel, [across, total], 4, 1, "far_product")
-    partials = multiply(other_kernel, [neighbour, total], 2, ZL * ROW, "other_product")
+    bottom, total = pl.pallas_call(
+        near_kernel,
+        out_shape=[staged, pltpu.VMEM((pairs, bra), jnp.float32)],
+        in_specs=[VMEM, VMEM, VMEM, HBM],
+        out_specs=[VMEM, VMEM],
+        scratch_shapes=[pltpu.SemaphoreType.DMA((PIECES,))],
+        compiler_params=params,
+        cost_estimate=pl.CostEstimate(
+            flops=pairs * integrals.size, bytes_accessed=2 * integrals.size, transcendentals=0
+        ),
+        name="near_product",
+    )(in_vmem(couple), in_vmem(swapped), in_vmem(top), in_hbm(integrals))
+    across = local(after_kernel, across.shape, across.dtype, [in_vmem(across), in_vmem(total)], name="after")
+    swapped = lax.ppermute(across, "core", core_swap)
+    total = multiply(far_kernel, [across, total, top, bottom], "far_product")
+    partials = multiply(last_kernel, [swapped, total, top, bottom], "last_product", (ZL * ROW,))
     shared = lax.all_to_all(partials, ("zl", "row"), 0, 0, tiled=True)
     out = pl.pallas_call(
         finish_kernel,

time: 49.4 us -> 48.2 us (0.976)
  waiting for transfers between devices: 7.78 us -> 5.74 us
  starting transfers between devices: 6.55 us -> 7.12 us
    ppermute x1, waiting for transfers between devices: 2.74 us -> 0.59 us  [per_device(): across = lax.ppermute(couple, 'x', [(i, X - 1 - i) for i in range(X)])]
    ppermute x1, starting transfers between devices: 2.18 us -> 2.85 us  [per_device(): across = lax.ppermute(couple, 'x', [(i, X - 1 - i) for i in range(X)])]
  transfers between devices with their start and end apart: 4 -> 5, of which waited for: 3 -> 4; matrix products, arithmetic and copies ran while one was open for 0% -> 0% of each run, Pallas kernels for 10% -> 11%
where the time goes in v3:
time: 48.2 us; the launch traced here: 47.3 us
  blocking collectives  26.9 us (56%)
  starting transfers between devices  7.12 us (15%)
  Pallas kernels  6.84 us (14%)
  waiting for transfers between devices  5.74 us (12%)
  local copies, waits for them, and re-layouts  0.61 us (1%)
    all_to_all x1, blocking collectives, per_device(): got = lax.all_to_all(sent, ('zh', 'zl'), 0, 0, tiled=True)  17.4 us
    all_to_all x1, blocking collectives, per_device(): shared = lax.all_to_all(partials, ('zl', 'row'), 0, 0, tiled=True)  9.53 us
    ppermute x1, waiting for transfers between devices, per_device(): return lax.ppermute(out, AXES, delivery_pairs())  4.36 us
    ppermute x1, starting transfers between devices, per_device(): across = lax.ppermute(couple, 'x', [(i, X - 1 - i) for i in range(X)])  2.85 us
    ppermute x1, starting transfers between devices, per_device(): return lax.ppermute(out, AXES, delivery_pairs())  2.69 us
    pallas_call x1, Pallas kernels, per_device(): pl.pallas_call(near_kernel, out_shape=[staged, pltpu.VMEM((pairs, bra), j...  2.28 us
    pallas_call x1, Pallas kernels, per_device(): pl.pallas_call(stage_top_kernel, out_shape=staged, in_specs=[HBM], out_sp...  2.21 us
    ppermute x1, starting transfers between devices, per_device(): beside = lax.ppermute(chosen, 'x', [(i, i ^ 1) for i in range(X)])  1.58 us
  transfers between devices with their start and end apart: 5, of which 4 were waited for; matrix products, arithmetic and copies ran while one was open for 0% of the time, Pallas kernels for 11%

profile of v3, /device:TPU:16, one launch (start us, length us, event | category | flops | bytes accessed | tf_op | source)
XLA Modules:
  0.0 47.3 jit_solution(15069598410339879966)
XLA Ops:
  0.0 0.9 %prepare.1 = (bf16[8,16,512]{2,1,0:T(8,128)(2,1)S(1)}, s32[2,8,16,128]{3,2,1,0:T(8,128)S(1)}, s32[2,16,128]{2,1,0:T(8,128)S(1)}) custom-call(s32[8]{0:T(128)} %partner_hbm.1, bf16[16,8,128]{2,1,0:T(8,128)(2,1)} %amplitudes_hbm.1), custom_call_target="tpu_custom_call" | custom-call | tf_op jit(solution)/shard_map/prepare/pallas_call | solution.py:210
  0.9 17.4 %all_to_all.10.got_ref = bf16[8,16,512]{2,1,0:T(8,128)(2,1)S(1)} all-to-all(bf16[8,16,512]{2,1,0:T(8,128)(2,1)S(1)} %get-tuple-element.12), channel_id=1, replica_groups=mesh['zh'=4,'zl'=2,'x'=4,'core'=2,'row'=4] {'zh','zl'}, dimensions={0} | all-to-all | bytes 262144 | tf_op jit(solution)/shard_map/all_to_all | solution.py:227
  18.3 1.6 %collective-permute-start = (bf16[2,16,512]{2,1,0:T(8,128)(2,1)S(1)}, bf16[2,16,512]{2,1,0:T(8,128)(2,1)S(1)}, u32[]{:S(2)}, u32[]{:S(2)}) collective-permute-start(bf16[2,16,512]{2,1,0:T(8,128)(2,1)S(1)} %choose.1), channel_id=1, source_target_pairs={{0,8},{8,0},{16,24},{24,16},{1,9},{9,1},{17,25},{25,17},{2,10},{10... | collective-permute-start | bytes 98312 | tf_op jit(solution)/shard_map/ppermute | solution.py:258
  19.9 2.2 %stage_top.1.rest_0_.top_ref = bf16[256,8192]{1,0:T(8,128)(2,1)S(1)} custom-call(bf16[512,8192]{1,0:T(8,128)(2,1)} %integrals_ref.3), custom_call_target="tpu_custom_call" | custom-call | bytes 8388608 | tf_op jit(solution)/shard_map/stage_top/pallas_call | solution.py:259
  22.1 0.2 collective-permute-done
  22.3 0.0 collective-permute-start.2
  22.3 2.8 %collective-permute-start.1 = (bf16[2,2,16,512]{3,2,1,0:T(8,128)(2,1)S(1)}, bf16[2,2,16,512]{3,2,1,0:T(8,128)(2,1)S(1)}, u32[]{:S(2)}, u32[]{:S(2)}) collective-permute-start(bf16[2,2,16,512]{3,2,1,0:T(8,128)(2,1)S(1)} %join.1.packed_ref), channel_id=1, source_target_pairs={{0,24},{8,16},{16,8},{24,0},{1,25},{9,17},{17,9},{25,1},{2,26},{10... | collective-permute-start | bytes 196616 | tf_op jit(solution)/shard_map/ppermute | solution.py:277
  25.1 0.0 collective-permute-done.2.swapped_ref
  25.1 2.3 %near_product.1 = (bf16[256,8192]{1,0:T(8,128)(2,1)S(1)}, f32[16,512]{1,0:T(8,128)S(1)}) custom-call(bf16[2,2,16,512]{3,2,1,0:T(8,128)(2,1)S(1)} %join.1.packed_ref, bf16[2,2,16,512]{3,2,1,0:T(8,128)(2,1)S(1)} %collective-permute-done.2.swapped_ref, bf16[256,8192]{1,0:T(8,128)(2,1)S(1)} %stage_top.1.rest_0_.top_ref, bf16[512,8192]{1,0:T(8,128)(2,1)} %integrals_ref.3), custom_call_target="tpu_custom_call" | custom-call | flops 67108864 | bytes 8388608 | tf_op jit(solution)/shard_map/near_product/pallas_call | solution.py:278
  27.4 0.6 %collective-permute-done.1.value_ref = bf16[2,2,16,512]{3,2,1,0:T(8,128)(2,1)S(1)} collective-permute-done((bf16[2,2,16,512]{3,2,1,0:T(8,128)(2,1)S(1)}, bf16[2,2,16,512]{3,2,1,0:T(8,128)(2,1)S(1)}, u32[]{:S(2)}, u32[]{:S(2)}) %collective-permute-start.1) | collective-permute-done | bytes 65568 | tf_op jit(solution)/shard_map/ppermute | solution.py:277
  28.0 0.0 collective-permute-start.3
  28.0 0.7 %far_product.1.before_ref = f32[16,512]{1,0:T(8,128)S(1)} custom-call(bf16[2,2,16,512]{3,2,1,0:T(8,128)(2,1)S(1)} %after.1.packed_ref, f32[16,512]{1,0:T(8,128)S(1)} %get-tuple-element.13.first_ref.before_ref, bf16[256,8192]{1,0:T(8,128)(2,1)S(1)} %stage_top.1.rest_0_.top_ref, bf16[256,8192]{1,0:T(8,128)(2,1)S(1)} %get-tuple-element.14.bottom_ref), custom_call_target="tpu_custom_call" | custom-call | flops 33554432 | bytes 2097152 | tf_op jit(solution)/shard_map/far_product/pallas_call | solution.py:239
  28.7 0.6 %collective-permute-done.3.packed_ref = bf16[2,2,16,512]{3,2,1,0:T(8,128)(2,1)S(1)} collective-permute-done((bf16[2,2,16,512]{3,2,1,0:T(8,128)(2,1)S(1)}, bf16[2,2,16,512]{3,2,1,0:T(8,128)(2,1)S(1)}, u32[]{:S(2)}, u32[]{:S(2)}) %collective-permute-start.3) | collective-permute-done | bytes 65568 | tf_op jit(solution)/shard_map/ppermute | solution.py:291
  29.3 0.7 %last_product.1 = f32[8,16,512]{2,1,0:T(8,128)S(1)} custom-call(bf16[2,2,16,512]{3,2,1,0:T(8,128)(2,1)S(1)} %collective-permute-done.3.packed_ref, f32[16,512]{1,0:T(8,128)S(1)} %far_product.1.before_ref, bf16[256,8192]{1,0:T(8,128)(2,1)S(1)} %stage_top.1.rest_0_.top_ref, bf16[256,8192]{1,0:T(8,128)(2,1)S(1)} %get-tuple-element.14.bottom_ref), custom_call_target="tpu_custom_call" | custom-call | flops 33554432 | bytes 2097152 | tf_op jit(solution)/shard_map/last_product/pallas_call | solution.py:239
  30.0 9.5 %all_to_all.11.shared_ref = f32[8,16,512]{2,1,0:T(8,128)S(1)} all-to-all(f32[8,16,512]{2,1,0:T(8,128)S(1)} %last_product.1), channel_id=1, replica_groups=mesh['zh'=4,'zl'=2,'x'=4,'core'=2,'row'=4] {'zl','row'}, dimensions={0} | all-to-all | bytes 524288 | tf_op jit(solution)/shard_map/all_to_all | solution.py:294
  39.5 0.1 finish.1
  39.6 2.7 %collective-permute-start.4 = (bf16[16,8,128]{2,1,0:T(8,128)(2,1)S(1)}, bf16[16,8,128]{2,1,0:T(8,128)(2,1)S(1)}, u32[]{:S(2)}, u32[]{:S(2)}) collective-permute-start(bf16[16,8,128]{2,1,0:T(8,128)(2,1)S(1)} %finish.1), channel_id=1, source_target_pairs={{0,160},{1,224},{2,0},{3,192},{4,164},{5,228},{6,4},{7,196},{8,168... | collective-permute-start | bytes 98312 | tf_op jit(solution)/shard_map/ppermute | solution.py:303
  42.3 4.4 %collective-permute-done.4 = bf16[16,8,128]{2,1,0:T(8,128)(2,1)S(1)} collective-permute-done((bf16[16,8,128]{2,1,0:T(8,128)(2,1)S(1)}, bf16[16,8,128]{2,1,0:T(8,128)(2,1)S(1)}, u32[]{:S(2)}, u32[]{:S(2)}) %collective-permute-start.4) | collective-permute-done | bytes 32800 | tf_op jit(solution)/shard_map/ppermute | solution.py:303
  46.6 0.6 %copy.5 = bf16[16,8,128]{2,1,0:T(8,128)(2,1)} copy(bf16[16,8,128]{2,1,0:T(8,128)(2,1)S(1)} %collective-permute-done.4) | data formatting | bytes 65536
  (3 shorter events, 0.1 us)
Async XLA Ops:
  18.3 4.0 %collective-permute-start = (bf16[2,16,512]{2,1,0:T(8,128)(2,1)S(1)}, bf16[2,16,512]{2,1,0:T(8,128)(2,1)S(1)}, u32[]{:S(2)}, u32[]{:S(2)}) collective-permute-start(bf16[2,16,512]{2,1,0:T(8,128)(2,1)S(1)} %choose.1), channel_id=1, source_target_pairs={{0,8},{8,0},{16,24},{24,16},{1,9},{9,1},{17,25},{25,17},{2,10},{10... | collective-permute-start | bytes 98312 | tf_op jit(solution)/shard_map/ppermute | solution.py:258
  22.3 2.9 %collective-permute-start.2 = (bf16[2,2,16,512]{3,2,1,0:T(8,128)(2,1)S(1)}, bf16[2,2,16,512]{3,2,1,0:T(8,128)(2,1)S(1)}, u32[]{:S(2)}, u32[]{:S(2)}) collective-permute-start(bf16[2,2,16,512]{3,2,1,0:T(8,128)(2,1)S(1)} %join.1.packed_ref), channel_id=1, source_target_pairs={{0,4},{4,0},{1,5},{5,1},{2,6},{6,2},{3,7},{7,3},{8,12},{12,8},{9,1... | collective-permute-start | bytes 196616 | tf_op jit(solution)/shard_map/ppermute | solution.py:276
  22.3 5.7 %collective-permute-start.1 = (bf16[2,2,16,512]{3,2,1,0:T(8,128)(2,1)S(1)}, bf16[2,2,16,512]{3,2,1,0:T(8,128)(2,1)S(1)}, u32[]{:S(2)}, u32[]{:S(2)}) collective-permute-start(bf16[2,2,16,512]{3,2,1,0:T(8,128)(2,1)S(1)} %join.1.packed_ref), channel_id=1, source_target_pairs={{0,24},{8,16},{16,8},{24,0},{1,25},{9,17},{17,9},{25,1},{2,26},{10... | collective-permute-start | bytes 196616 | tf_op jit(solution)/shard_map/ppermute | solution.py:277
  28.0 1.3 %collective-permute-start.3 = (bf16[2,2,16,512]{3,2,1,0:T(8,128)(2,1)S(1)}, bf16[2,2,16,512]{3,2,1,0:T(8,128)(2,1)S(1)}, u32[]{:S(2)}, u32[]{:S(2)}) collective-permute-start(bf16[2,2,16,512]{3,2,1,0:T(8,128)(2,1)S(1)} %after.1.packed_ref), channel_id=1, source_target_pairs={{0,4},{4,0},{1,5},{5,1},{2,6},{6,2},{3,7},{7,3},{8,12},{12,8},{9,1... | collective-permute-start | bytes 196616 | tf_op jit(solution)/shard_map/ppermute | solution.py:291
  39.6 7.1 %collective-permute-start.4 = (bf16[16,8,128]{2,1,0:T(8,128)(2,1)S(1)}, bf16[16,8,128]{2,1,0:T(8,128)(2,1)S(1)}, u32[]{:S(2)}, u32[]{:S(2)}) collective-permute-start(bf16[16,8,128]{2,1,0:T(8,128)(2,1)S(1)} %finish.1), channel_id=1, source_target_pairs={{0,160},{1,224},{2,0},{3,192},{4,164},{5,228},{6,4},{7,196},{8,168... | collective-permute-start | bytes 98312 | tf_op jit(solution)/shard_map/ppermute | solution.py:303

commit v4 on v3

--- a/solution.py
+++ b/solution.py
@@ -11,7 +11,7 @@
 TILES = ZH * ZL
 AXES = ("zh", "zl", "x", "core", "row")
 PIECES = 8
-REACH = (3, 1, 0, 2)
+REACH = (3, 0, 1, 2)
 VMEM = pl.BlockSpec(memory_space=pltpu.VMEM)
 HBM = pl.BlockSpec(memory_space=pltpu.HBM)
 
@@ -56,7 +56,9 @@
         copy.wait()
 
 
-def prepare_kernel(partner_hbm, amplitudes_hbm, sent_ref, pick_ref, keep_ref, partner_ref, amplitudes_ref, sems):
+def prepare_kernel(
+    partner_hbm, amplitudes_hbm, sent_ref, pick_ref, odd_ref, place_ref, partner_ref, amplitudes_ref, sems
+):
     fetch(
         [
             pltpu.make_async_copy(partner_hbm, partner_ref, sems.at[0]),
@@ -72,9 +74,10 @@
     off = jnp.where(turn == 0, REACH[0], jnp.where(turn == 1, REACH[1], jnp.where(turn == 2, REACH[2], REACH[3])))
     target = jnp.where(zl == 0, 2 * zh - off + TILES, 2 * zh + 1 + off) % TILES
     bra = partner_ref[target]
+    odd_ref[...] = jnp.full(odd_ref.shape, bra % 2, jnp.int32)
+    z = zh * ZL + zl
     for h in range(2):
-        keep_ref[h] = jnp.full(keep_ref.shape[1:], jnp.where(bra == 2 * zh + h, 1, 0), jnp.int32)
-    z = zh * ZL + zl
+        place_ref[h] = jnp.full(place_ref.shape[1:], jnp.where(partner_ref[z] == 2 * row + h, 1, 0), jnp.int32)
     upper = partner_ref[z] % 2 == 1
     rows = jnp.swapaxes(amplitudes_ref[...].astype(jnp.float32), 0, 1)
     units, pairs, _ = rows.shape
@@ -182,23 +185,29 @@
         out_ref[j] = total
 
 
-def finish_kernel(keep_ref, shared_ref, out_ref):
-    pairs, width = shared_ref.shape[1:]
+def finish_kernel(odd_ref, shared_ref, out_ref):
+    odd = jnp.concatenate([odd_ref[...]] * (out_ref.shape[1] // odd_ref.shape[1]), axis=1) != 0
     sums = []
     for h in range(2):
         total = shared_ref[h * ROW]
         for j in range(1, ROW):
             total = total + shared_ref[h * ROW + j]
-        wanted = jnp.concatenate([keep_ref[h]] * (width // keep_ref.shape[2]), axis=1) != 0
-        total = jnp.where(wanted, total, 0.0)
-        sums.append(total.astype(jnp.bfloat16).astype(jnp.float32))
+        sums.append(total)
+    out_ref[...] = jnp.where(odd, sums[1], sums[0]).astype(out_ref.dtype)
+
+
+def place_kernel(place_ref, block_ref, out_ref):
+    block = block_ref[...].astype(jnp.float32)
+    pairs, width = block.shape
     lower = lower_lanes(pairs)
+    left = lower & (place_ref[0] != 0)
+    right = jnp.logical_not(lower) & (place_ref[1] != 0)
     rows = []
     for j in range(width // (2 * TS)):
-        part = slice(j * 2 * TS, (j + 1) * 2 * TS)
-        left, right = sums[0][:, part], sums[1][:, part]
-        rows.append(jnp.where(lower, left, pltpu.roll(right, TS, 1)))
-        rows.append(jnp.where(lower, pltpu.roll(left, TS, 1), right))
+        part = block[:, j * 2 * TS : (j + 1) * 2 * TS]
+        turned = pltpu.roll(part, TS, 1)
+        rows.append(jnp.where(left, part, jnp.where(right, turned, 0.0)))
+        rows.append(jnp.where(left, turned, jnp.where(right, part, 0.0)))
     out_ref[...] = jnp.swapaxes(jnp.stack(rows, 0), 0, 1).astype(out_ref.dtype)
 
 
@@ -207,15 +216,16 @@
     width = rows_dev * TS
     bra = integrals.shape[0]
     params = pltpu.CompilerParams(vmem_limit_bytes=4 * 1024 * 1024)
-    sent, pick, keep = pl.pallas_call(
+    sent, pick, odd, place = pl.pallas_call(
         prepare_kernel,
         out_shape=[
             pltpu.VMEM((TILES, pairs, width), jnp.bfloat16),
             pltpu.VMEM((2, TILES, pairs, 128), jnp.int32),
+            pltpu.VMEM((pairs, 128), jnp.int32),
             pltpu.VMEM((2, pairs, 128), jnp.int32),
         ],
         in_specs=[HBM, HBM],
-        out_specs=[VMEM, VMEM, VMEM],
+        out_specs=[VMEM, VMEM, VMEM, VMEM],
         scratch_shapes=[
             pltpu.SMEM(partner.shape, partner.dtype),
             pltpu.VMEM(amplitudes.shape, amplitudes.dtype),
@@ -292,15 +302,23 @@
     total = multiply(far_kernel, [across, total, top, bottom], "far_product")
     partials = multiply(last_kernel, [swapped, total, top, bottom], "last_product", (ZL * ROW,))
     shared = lax.all_to_all(partials, ("zl", "row"), 0, 0, tiled=True)
-    out = pl.pallas_call(
+    block = pl.pallas_call(
         finish_kernel,
-        out_shape=pltpu.VMEM(amplitudes.shape, jnp.bfloat16),
+        out_shape=pltpu.VMEM((pairs, bra), jnp.bfloat16),
         in_specs=[VMEM, VMEM],
         out_specs=VMEM,
         compiler_params=params,
         name="finish",
-    )(in_vmem(keep), in_vmem(shared))
-    return lax.ppermute(out, AXES, delivery_pairs())
+    )(in_vmem(odd), in_vmem(shared))
+    block = lax.ppermute(block, AXES, delivery_pairs())
+    return pl.pallas_call(
+        place_kernel,
+        out_shape=jax.ShapeDtypeStruct(amplitudes.shape, jnp.bfloat16),
+        in_specs=[VMEM, VMEM],
+        out_specs=VMEM,
+        compiler_params=params,
+        name="place",
+    )(in_vmem(place), in_vmem(block))
 
 
 def solution(mesh):

time: 48.2 us -> 47.9 us (level)
  starting transfers between devices: 7.12 us -> 6.46 us
  Pallas kernels: 6.84 us -> 7.46 us
  local copies, waits for them, and re-layouts: 0.61 us -> 0 us
    ppermute x1, starting transfers between devices: 2.69 us -> 2.03 us  [per_device(): block = lax.ppermute(block, AXES, delivery_pairs())]
    pallas_call x1 -> x2, Pallas kernels: 0.1 us -> 0.72 us  [the longest x1 0.7 us: per_device(): pl.pallas_call(place_kernel, out_shape=jax.ShapeDtypeStruct(amplitudes.sh...]
    unnamed x1 -> x0, local copies, waits for them, and re-layouts: 0.61 us -> none
where the time goes in v4:
time: 47.9 us; the launch traced here: 47 us
  blocking collectives  26.9 us (56%)
  Pallas kernels  7.46 us (16%)
  starting transfers between devices  6.46 us (13%)
  waiting for transfers between devices  6.17 us (13%)
    all_to_all x1, blocking collectives, per_device(): got = lax.all_to_all(sent, ('zh', 'zl'), 0, 0, tiled=True)  17.4 us
    all_to_all x1, blocking collectives, per_device(): shared = lax.all_to_all(partials, ('zl', 'row'), 0, 0, tiled=True)  9.53 us
    ppermute x1, waiting for transfers between devices, per_device(): block = lax.ppermute(block, AXES, delivery_pairs())  4.79 us
    ppermute x1, starting transfers between devices, per_device(): across = lax.ppermute(couple, 'x', [(i, X - 1 - i) for i in range(X)])  2.85 us
    pallas_call x1, Pallas kernels, per_device(): pl.pallas_call(near_kernel, out_shape=[staged, pltpu.VMEM((pairs, bra), j...  2.28 us
    pallas_call x1, Pallas kernels, per_device(): pl.pallas_call(stage_top_kernel, out_shape=staged, in_specs=[HBM], out_sp...  2.21 us
    ppermute x1, starting transfers between devices, per_device(): block = lax.ppermute(block, AXES, delivery_pairs())  2.03 us
    ppermute x1, starting transfers between devices, per_device(): beside = lax.ppermute(chosen, 'x', [(i, i ^ 1) for i in range(X)])  1.58 us
  transfers between devices with their start and end apart: 5, of which 4 were waited for; matrix products, arithmetic and copies ran while one was open for 0% of the time, Pallas kernels for 11%

profile of v4, /device:TPU:16, one launch (start us, length us, event | category | flops | bytes accessed | tf_op | source)
XLA Modules:
  0.0 47.0 jit_solution(5855095112232173201)
XLA Ops:
  0.0 0.9 %prepare.1 = (bf16[8,16,512]{2,1,0:T(8,128)(2,1)S(1)}, s32[2,8,16,128]{3,2,1,0:T(8,128)S(1)}, s32[16,128]{1,0:T(8,128)S(1)}, s32[2,16,128]{2,1,0:T(8,128)S(1)}) custom-call(s32[8]{0:T(128)} %partner_hbm.1, bf16[16,8,128]{2,1,0:T(8,128)(2,1)} %amplitudes_hbm.1), custom_call_target="tpu_custom_call" | custom-call | tf_op jit(solution)/shard_map/prepare/pallas_call | solution.py:219
  0.9 17.4 %all_to_all.10.got_ref = bf16[8,16,512]{2,1,0:T(8,128)(2,1)S(1)} all-to-all(bf16[8,16,512]{2,1,0:T(8,128)(2,1)S(1)} %get-tuple-element.14), channel_id=1, replica_groups=mesh['zh'=4,'zl'=2,'x'=4,'core'=2,'row'=4] {'zh','zl'}, dimensions={0} | all-to-all | bytes 262144 | tf_op jit(solution)/shard_map/all_to_all | solution.py:237
  18.3 1.6 %collective-permute-start = (bf16[2,16,512]{2,1,0:T(8,128)(2,1)S(1)}, bf16[2,16,512]{2,1,0:T(8,128)(2,1)S(1)}, u32[]{:S(2)}, u32[]{:S(2)}) collective-permute-start(bf16[2,16,512]{2,1,0:T(8,128)(2,1)S(1)} %choose.1), channel_id=1, source_target_pairs={{0,8},{8,0},{16,24},{24,16},{1,9},{9,1},{17,25},{25,17},{2,10},{10... | collective-permute-start | bytes 98312 | tf_op jit(solution)/shard_map/ppermute | solution.py:268
  19.9 2.2 %stage_top.1.rest_0_.top_ref = bf16[256,8192]{1,0:T(8,128)(2,1)S(1)} custom-call(bf16[512,8192]{1,0:T(8,128)(2,1)} %integrals_ref.3), custom_call_target="tpu_custom_call" | custom-call | bytes 8388608 | tf_op jit(solution)/shard_map/stage_top/pallas_call | solution.py:269
  22.1 0.2 collective-permute-done
  22.3 0.0 collective-permute-start.2
  22.3 2.8 %collective-permute-start.1 = (bf16[2,2,16,512]{3,2,1,0:T(8,128)(2,1)S(1)}, bf16[2,2,16,512]{3,2,1,0:T(8,128)(2,1)S(1)}, u32[]{:S(2)}, u32[]{:S(2)}) collective-permute-start(bf16[2,2,16,512]{3,2,1,0:T(8,128)(2,1)S(1)} %join.1.packed_ref), channel_id=1, source_target_pairs={{0,24},{8,16},{16,8},{24,0},{1,25},{9,17},{17,9},{25,1},{2,26},{10... | collective-permute-start | bytes 196616 | tf_op jit(solution)/shard_map/ppermute | solution.py:287
  25.1 0.0 collective-permute-done.2.swapped_ref
  25.1 2.3 %near_product.1 = (bf16[256,8192]{1,0:T(8,128)(2,1)S(1)}, f32[16,512]{1,0:T(8,128)S(1)}) custom-call(bf16[2,2,16,512]{3,2,1,0:T(8,128)(2,1)S(1)} %join.1.packed_ref, bf16[2,2,16,512]{3,2,1,0:T(8,128)(2,1)S(1)} %collective-permute-done.2.swapped_ref, bf16[256,8192]{1,0:T(8,128)(2,1)S(1)} %stage_top.1.rest_0_.top_ref, bf16[512,8192]{1,0:T(8,128)(2,1)} %integrals_ref.3), custom_call_target="tpu_custom_call" | custom-call | flops 67108864 | bytes 8388608 | tf_op jit(solution)/shard_map/near_product/pallas_call | solution.py:288
  27.4 0.6 %collective-permute-done.1.value_ref = bf16[2,2,16,512]{3,2,1,0:T(8,128)(2,1)S(1)} collective-permute-done((bf16[2,2,16,512]{3,2,1,0:T(8,128)(2,1)S(1)}, bf16[2,2,16,512]{3,2,1,0:T(8,128)(2,1)S(1)}, u32[]{:S(2)}, u32[]{:S(2)}) %collective-permute-start.1) | collective-permute-done | bytes 65568 | tf_op jit(solution)/shard_map/ppermute | solution.py:287
  28.0 0.0 collective-permute-start.3
  28.0 0.7 %far_product.1.before_ref = f32[16,512]{1,0:T(8,128)S(1)} custom-call(bf16[2,2,16,512]{3,2,1,0:T(8,128)(2,1)S(1)} %after.1.packed_ref, f32[16,512]{1,0:T(8,128)S(1)} %get-tuple-element.15.first_ref.before_ref, bf16[256,8192]{1,0:T(8,128)(2,1)S(1)} %stage_top.1.rest_0_.top_ref, bf16[256,8192]{1,0:T(8,128)(2,1)S(1)} %get-tuple-element.16.bottom_ref), custom_call_target="tpu_custom_call" | custom-call | flops 33554432 | bytes 2097152 | tf_op jit(solution)/shard_map/far_product/pallas_call | solution.py:249
  28.7 0.6 %collective-permute-done.3.packed_ref = bf16[2,2,16,512]{3,2,1,0:T(8,128)(2,1)S(1)} collective-permute-done((bf16[2,2,16,512]{3,2,1,0:T(8,128)(2,1)S(1)}, bf16[2,2,16,512]{3,2,1,0:T(8,128)(2,1)S(1)}, u32[]{:S(2)}, u32[]{:S(2)}) %collective-permute-start.3) | collective-permute-done | bytes 65568 | tf_op jit(solution)/shard_map/ppermute | solution.py:301
  29.3 0.7 %last_product.1 = f32[8,16,512]{2,1,0:T(8,128)S(1)} custom-call(bf16[2,2,16,512]{3,2,1,0:T(8,128)(2,1)S(1)} %collective-permute-done.3.packed_ref, f32[16,512]{1,0:T(8,128)S(1)} %far_product.1.before_ref, bf16[256,8192]{1,0:T(8,128)(2,1)S(1)} %stage_top.1.rest_0_.top_ref, bf16[256,8192]{1,0:T(8,128)(2,1)S(1)} %get-tuple-element.16.bottom_ref), custom_call_target="tpu_custom_call" | custom-call | flops 33554432 | bytes 2097152 | tf_op jit(solution)/shard_map/last_product/pallas_call | solution.py:249
  30.0 9.5 %all_to_all.11.shared_ref = f32[8,16,512]{2,1,0:T(8,128)S(1)} all-to-all(f32[8,16,512]{2,1,0:T(8,128)S(1)} %last_product.1), channel_id=1, replica_groups=mesh['zh'=4,'zl'=2,'x'=4,'core'=2,'row'=4] {'zl','row'}, dimensions={0} | all-to-all | bytes 524288 | tf_op jit(solution)/shard_map/all_to_all | solution.py:304
  39.5 2.0 %collective-permute-start.4 = (bf16[16,512]{1,0:T(8,128)(2,1)S(1)}, bf16[16,512]{1,0:T(8,128)(2,1)S(1)}, u32[]{:S(2)}, u32[]{:S(2)}) collective-permute-start(bf16[16,512]{1,0:T(8,128)(2,1)S(1)} %finish.1), channel_id=1, source_target_pairs={{0,160},{1,0},{2,224},{3,192},{4,164},{5,4},{6,228},{7,196},{8,168... | collective-permute-start | bytes 49160 | tf_op jit(solution)/shard_map/ppermute | solution.py:313
  41.5 4.8 %collective-permute-done.4.block_ref = bf16[16,512]{1,0:T(8,128)(2,1)S(1)} collective-permute-done((bf16[16,512]{1,0:T(8,128)(2,1)S(1)}, bf16[16,512]{1,0:T(8,128)(2,1)S(1)}, u32[]{:S(2)}, u32[]{:S(2)}) %collective-permute-start.4) | collective-permute-done | bytes 16416 | tf_op jit(solution)/shard_map/ppermute | solution.py:313
  46.3 0.7 %place.1 = bf16[16,8,128]{2,1,0:T(8,128)(2,1)} custom-call(s32[2,16,128]{2,1,0:T(8,128)S(1)} %get-tuple-element.11.place_ref, bf16[16,512]{1,0:T(8,128)(2,1)S(1)} %collective-permute-done.4.block_ref), custom_call_target="tpu_custom_call" | custom-call | tf_op jit(solution)/shard_map/place/pallas_call | solution.py:314
  (4 shorter events, 0.1 us)
Async XLA Ops:
  18.3 4.0 %collective-permute-start = (bf16[2,16,512]{2,1,0:T(8,128)(2,1)S(1)}, bf16[2,16,512]{2,1,0:T(8,128)(2,1)S(1)}, u32[]{:S(2)}, u32[]{:S(2)}) collective-permute-start(bf16[2,16,512]{2,1,0:T(8,128)(2,1)S(1)} %choose.1), channel_id=1, source_target_pairs={{0,8},{8,0},{16,24},{24,16},{1,9},{9,1},{17,25},{25,17},{2,10},{10... | collective-permute-start | bytes 98312 | tf_op jit(solution)/shard_map/ppermute | solution.py:268
  22.3 2.9 %collective-permute-start.2 = (bf16[2,2,16,512]{3,2,1,0:T(8,128)(2,1)S(1)}, bf16[2,2,16,512]{3,2,1,0:T(8,128)(2,1)S(1)}, u32[]{:S(2)}, u32[]{:S(2)}) collective-permute-start(bf16[2,2,16,512]{3,2,1,0:T(8,128)(2,1)S(1)} %join.1.packed_ref), channel_id=1, source_target_pairs={{0,4},{4,0},{1,5},{5,1},{2,6},{6,2},{3,7},{7,3},{8,12},{12,8},{9,1... | collective-permute-start | bytes 196616 | tf_op jit(solution)/shard_map/ppermute | solution.py:286
  22.3 5.7 %collective-permute-start.1 = (bf16[2,2,16,512]{3,2,1,0:T(8,128)(2,1)S(1)}, bf16[2,2,16,512]{3,2,1,0:T(8,128)(2,1)S(1)}, u32[]{:S(2)}, u32[]{:S(2)}) collective-permute-start(bf16[2,2,16,512]{3,2,1,0:T(8,128)(2,1)S(1)} %join.1.packed_ref), channel_id=1, source_target_pairs={{0,24},{8,16},{16,8},{24,0},{1,25},{9,17},{17,9},{25,1},{2,26},{10... | collective-permute-start | bytes 196616 | tf_op jit(solution)/shard_map/ppermute | solution.py:287
  28.0 1.3 %collective-permute-start.3 = (bf16[2,2,16,512]{3,2,1,0:T(8,128)(2,1)S(1)}, bf16[2,2,16,512]{3,2,1,0:T(8,128)(2,1)S(1)}, u32[]{:S(2)}, u32[]{:S(2)}) collective-permute-start(bf16[2,2,16,512]{3,2,1,0:T(8,128)(2,1)S(1)} %after.1.packed_ref), channel_id=1, source_target_pairs={{0,4},{4,0},{1,5},{5,1},{2,6},{6,2},{3,7},{7,3},{8,12},{12,8},{9,1... | collective-permute-start | bytes 196616 | tf_op jit(solution)/shard_map/ppermute | solution.py:301
  39.5 6.8 %collective-permute-start.4 = (bf16[16,512]{1,0:T(8,128)(2,1)S(1)}, bf16[16,512]{1,0:T(8,128)(2,1)S(1)}, u32[]{:S(2)}, u32[]{:S(2)}) collective-permute-start(bf16[16,512]{1,0:T(8,128)(2,1)S(1)} %finish.1), channel_id=1, source_target_pairs={{0,160},{1,0},{2,224},{3,192},{4,164},{5,4},{6,228},{7,196},{8,168... | collective-permute-start | bytes 49160 | tf_op jit(solution)/shard_map/ppermute | solution.py:313

commit v5 on v4

--- a/solution.py
+++ b/solution.py
@@ -11,14 +11,19 @@
 TILES = ZH * ZL
 AXES = ("zh", "zl", "x", "core", "row")
 PIECES = 8
-REACH = (3, 0, 1, 2)
+TARGETS = (
+    (5, 0, 7, 6, 4, 1, 2, 3),
+    (1, 0, 7, 2, 5, 6, 3, 4),
+    (3, 2, 1, 4, 6, 7, 0, 5),
+    (5, 4, 3, 2, 7, 6, 0, 1),
+)
+PACKED_TARGETS = tuple(sum(z << (3 * i) for i, z in enumerate(line)) for line in TARGETS)
 VMEM = pl.BlockSpec(memory_space=pltpu.VMEM)
 HBM = pl.BlockSpec(memory_space=pltpu.HBM)
 
 
 def target_z(zh, zl, row):
-    off = REACH[(row - zh) % ROW]
-    return (2 * zh - off) % TILES if zl == 0 else (2 * zh + 1 + off) % TILES
+    return TARGETS[zh][zl * ROW + row]
 
 
 def linear(zh, zl, x, core, row):
@@ -70,9 +75,9 @@
         source = partner_ref[2 * row + h]
         for z in range(TILES):
             pick_ref[h, z] = jnp.full(pick_ref.shape[2:], jnp.where(source == z, 1, 0), jnp.int32)
-    turn = (row - zh + ROW) % ROW
-    off = jnp.where(turn == 0, REACH[0], jnp.where(turn == 1, REACH[1], jnp.where(turn == 2, REACH[2], REACH[3])))
-    target = jnp.where(zl == 0, 2 * zh - off + TILES, 2 * zh + 1 + off) % TILES
+    packed = jnp.where(zh == 0, PACKED_TARGETS[0], PACKED_TARGETS[1])
+    packed = jnp.where(zh == 2, PACKED_TARGETS[2], jnp.where(zh == 3, PACKED_TARGETS[3], packed))
+    target = lax.shift_right_logical(packed, 3 * (zl * ROW + row)) & (TILES - 1)
     bra = partner_ref[target]
     odd_ref[...] = jnp.full(odd_ref.shape, bra % 2, jnp.int32)
     z = zh * ZL + zl

time: 47.9 us -> 47.3 us (0.987); the launches traced: 47 us -> 47 us
  no operation moved by 1% of the time
where the time goes in v5:
time: 47.3 us; the launch traced here: 47 us
  blocking collectives  26.9 us (57%)
  Pallas kernels  7.46 us (16%)
  starting transfers between devices  6.46 us (14%)
  waiting for transfers between devices  6.17 us (13%)
    all_to_all x1, blocking collectives, per_device(): got = lax.all_to_all(sent, ('zh', 'zl'), 0, 0, tiled=True)  17.4 us
    all_to_all x1, blocking collectives, per_device(): shared = lax.all_to_all(partials, ('zl', 'row'), 0, 0, tiled=True)  9.53 us
    ppermute x1, waiting for transfers between devices, per_device(): block = lax.ppermute(block, AXES, delivery_pairs())  4.79 us
    ppermute x1, starting transfers between devices, per_device(): across = lax.ppermute(couple, 'x', [(i, X - 1 - i) for i in range(X)])  2.85 us
    pallas_call x1, Pallas kernels, per_device(): pl.pallas_call(near_kernel, out_shape=[staged, pltpu.VMEM((pairs, bra), j...  2.28 us
    pallas_call x1, Pallas kernels, per_device(): pl.pallas_call(stage_top_kernel, out_shape=staged, in_specs=[HBM], out_sp...  2.21 us
    ppermute x1, starting transfers between devices, per_device(): block = lax.ppermute(block, AXES, delivery_pairs())  2.03 us
    ppermute x1, starting transfers between devices, per_device(): beside = lax.ppermute(chosen, 'x', [(i, i ^ 1) for i in range(X)])  1.58 us
  transfers between devices with their start and end apart: 5, of which 4 were waited for; matrix products, arithmetic and copies ran while one was open for 0% of the time, Pallas kernels for 11%

profile of v5, /device:TPU:16, one launch (start us, length us, event | category | flops | bytes accessed | tf_op | source)
XLA Modules:
  0.0 47.0 jit_solution(7408119338433925781)
XLA Ops:
  0.0 0.9 %prepare.1 = (bf16[8,16,512]{2,1,0:T(8,128)(2,1)S(1)}, s32[2,8,16,128]{3,2,1,0:T(8,128)S(1)}, s32[16,128]{1,0:T(8,128)S(1)}, s32[2,16,128]{2,1,0:T(8,128)S(1)}) custom-call(s32[8]{0:T(128)} %partner_hbm.1, bf16[16,8,128]{2,1,0:T(8,128)(2,1)} %amplitudes_hbm.1), custom_call_target="tpu_custom_call" | custom-call | tf_op jit(solution)/shard_map/prepare/pallas_call | solution.py:224
  0.9 17.4 %all_to_all.10.got_ref = bf16[8,16,512]{2,1,0:T(8,128)(2,1)S(1)} all-to-all(bf16[8,16,512]{2,1,0:T(8,128)(2,1)S(1)} %get-tuple-element.14), channel_id=1, replica_groups=mesh['zh'=4,'zl'=2,'x'=4,'core'=2,'row'=4] {'zh','zl'}, dimensions={0} | all-to-all | bytes 262144 | tf_op jit(solution)/shard_map/all_to_all | solution.py:242
  18.3 1.6 %collective-permute-start = (bf16[2,16,512]{2,1,0:T(8,128)(2,1)S(1)}, bf16[2,16,512]{2,1,0:T(8,128)(2,1)S(1)}, u32[]{:S(2)}, u32[]{:S(2)}) collective-permute-start(bf16[2,16,512]{2,1,0:T(8,128)(2,1)S(1)} %choose.1), channel_id=1, source_target_pairs={{0,8},{8,0},{16,24},{24,16},{1,9},{9,1},{17,25},{25,17},{2,10},{10... | collective-permute-start | bytes 98312 | tf_op jit(solution)/shard_map/ppermute | solution.py:273
  19.9 2.2 %stage_top.1.rest_0_.top_ref = bf16[256,8192]{1,0:T(8,128)(2,1)S(1)} custom-call(bf16[512,8192]{1,0:T(8,128)(2,1)} %integrals_ref.3), custom_call_target="tpu_custom_call" | custom-call | bytes 8388608 | tf_op jit(solution)/shard_map/stage_top/pallas_call | solution.py:274
  22.1 0.2 collective-permute-done
  22.3 0.0 collective-permute-start.2
  22.3 2.8 %collective-permute-start.1 = (bf16[2,2,16,512]{3,2,1,0:T(8,128)(2,1)S(1)}, bf16[2,2,16,512]{3,2,1,0:T(8,128)(2,1)S(1)}, u32[]{:S(2)}, u32[]{:S(2)}) collective-permute-start(bf16[2,2,16,512]{3,2,1,0:T(8,128)(2,1)S(1)} %join.1.packed_ref), channel_id=1, source_target_pairs={{0,24},{8,16},{16,8},{24,0},{1,25},{9,17},{17,9},{25,1},{2,26},{10... | collective-permute-start | bytes 196616 | tf_op jit(solution)/shard_map/ppermute | solution.py:292
  25.1 0.0 collective-permute-done.2.swapped_ref
  25.1 2.3 %near_product.1 = (bf16[256,8192]{1,0:T(8,128)(2,1)S(1)}, f32[16,512]{1,0:T(8,128)S(1)}) custom-call(bf16[2,2,16,512]{3,2,1,0:T(8,128)(2,1)S(1)} %join.1.packed_ref, bf16[2,2,16,512]{3,2,1,0:T(8,128)(2,1)S(1)} %collective-permute-done.2.swapped_ref, bf16[256,8192]{1,0:T(8,128)(2,1)S(1)} %stage_top.1.rest_0_.top_ref, bf16[512,8192]{1,0:T(8,128)(2,1)} %integrals_ref.3), custom_call_target="tpu_custom_call" | custom-call | flops 67108864 | bytes 8388608 | tf_op jit(solution)/shard_map/near_product/pallas_call | solution.py:293
  27.4 0.6 %collective-permute-done.1.value_ref = bf16[2,2,16,512]{3,2,1,0:T(8,128)(2,1)S(1)} collective-permute-done((bf16[2,2,16,512]{3,2,1,0:T(8,128)(2,1)S(1)}, bf16[2,2,16,512]{3,2,1,0:T(8,128)(2,1)S(1)}, u32[]{:S(2)}, u32[]{:S(2)}) %collective-permute-start.1) | collective-permute-done | bytes 65568 | tf_op jit(solution)/shard_map/ppermute | solution.py:292
  28.0 0.0 collective-permute-start.3
  28.0 0.7 %far_product.1.before_ref = f32[16,512]{1,0:T(8,128)S(1)} custom-call(bf16[2,2,16,512]{3,2,1,0:T(8,128)(2,1)S(1)} %after.1.packed_ref, f32[16,512]{1,0:T(8,128)S(1)} %get-tuple-element.15.first_ref.before_ref, bf16[256,8192]{1,0:T(8,128)(2,1)S(1)} %stage_top.1.rest_0_.top_ref, bf16[256,8192]{1,0:T(8,128)(2,1)S(1)} %get-tuple-element.16.bottom_ref), custom_call_target="tpu_custom_call" | custom-call | flops 33554432 | bytes 2097152 | tf_op jit(solution)/shard_map/far_product/pallas_call | solution.py:254
  28.7 0.6 %collective-permute-done.3.packed_ref = bf16[2,2,16,512]{3,2,1,0:T(8,128)(2,1)S(1)} collective-permute-done((bf16[2,2,16,512]{3,2,1,0:T(8,128)(2,1)S(1)}, bf16[2,2,16,512]{3,2,1,0:T(8,128)(2,1)S(1)}, u32[]{:S(2)}, u32[]{:S(2)}) %collective-permute-start.3) | collective-permute-done | bytes 65568 | tf_op jit(solution)/shard_map/ppermute | solution.py:306
  29.3 0.7 %last_product.1 = f32[8,16,512]{2,1,0:T(8,128)S(1)} custom-call(bf16[2,2,16,512]{3,2,1,0:T(8,128)(2,1)S(1)} %collective-permute-done.3.packed_ref, f32[16,512]{1,0:T(8,128)S(1)} %far_product.1.before_ref, bf16[256,8192]{1,0:T(8,128)(2,1)S(1)} %stage_top.1.rest_0_.top_ref, bf16[256,8192]{1,0:T(8,128)(2,1)S(1)} %get-tuple-element.16.bottom_ref), custom_call_target="tpu_custom_call" | custom-call | flops 33554432 | bytes 2097152 | tf_op jit(solution)/shard_map/last_product/pallas_call | solution.py:254
  30.0 9.5 %all_to_all.11.shared_ref = f32[8,16,512]{2,1,0:T(8,128)S(1)} all-to-all(f32[8,16,512]{2,1,0:T(8,128)S(1)} %last_product.1), channel_id=1, replica_groups=mesh['zh'=4,'zl'=2,'x'=4,'core'=2,'row'=4] {'zl','row'}, dimensions={0} | all-to-all | bytes 524288 | tf_op jit(solution)/shard_map/all_to_all | solution.py:309
  39.5 2.0 %collective-permute-start.4 = (bf16[16,512]{1,0:T(8,128)(2,1)S(1)}, bf16[16,512]{1,0:T(8,128)(2,1)S(1)}, u32[]{:S(2)}, u32[]{:S(2)}) collective-permute-start(bf16[16,512]{1,0:T(8,128)(2,1)S(1)} %finish.1), channel_id=1, source_target_pairs={{0,160},{1,0},{2,224},{3,192},{4,164},{5,4},{6,228},{7,196},{8,168... | collective-permute-start | bytes 49160 | tf_op jit(solution)/shard_map/ppermute | solution.py:318
  41.5 4.8 %collective-permute-done.4.block_ref = bf16[16,512]{1,0:T(8,128)(2,1)S(1)} collective-permute-done((bf16[16,512]{1,0:T(8,128)(2,1)S(1)}, bf16[16,512]{1,0:T(8,128)(2,1)S(1)}, u32[]{:S(2)}, u32[]{:S(2)}) %collective-permute-start.4) | collective-permute-done | bytes 16416 | tf_op jit(solution)/shard_map/ppermute | solution.py:318
  46.3 0.7 %place.1 = bf16[16,8,128]{2,1,0:T(8,128)(2,1)} custom-call(s32[2,16,128]{2,1,0:T(8,128)S(1)} %get-tuple-element.11.place_ref, bf16[16,512]{1,0:T(8,128)(2,1)S(1)} %collective-permute-done.4.block_ref), custom_call_target="tpu_custom_call" | custom-call | tf_op jit(solution)/shard_map/place/pallas_call | solution.py:319
  (4 shorter events, 0.1 us)
Async XLA Ops:
  18.3 4.0 %collective-permute-start = (bf16[2,16,512]{2,1,0:T(8,128)(2,1)S(1)}, bf16[2,16,512]{2,1,0:T(8,128)(2,1)S(1)}, u32[]{:S(2)}, u32[]{:S(2)}) collective-permute-start(bf16[2,16,512]{2,1,0:T(8,128)(2,1)S(1)} %choose.1), channel_id=1, source_target_pairs={{0,8},{8,0},{16,24},{24,16},{1,9},{9,1},{17,25},{25,17},{2,10},{10... | collective-permute-start | bytes 98312 | tf_op jit(solution)/shard_map/ppermute | solution.py:273
  22.3 2.9 %collective-permute-start.2 = (bf16[2,2,16,512]{3,2,1,0:T(8,128)(2,1)S(1)}, bf16[2,2,16,512]{3,2,1,0:T(8,128)(2,1)S(1)}, u32[]{:S(2)}, u32[]{:S(2)}) collective-permute-start(bf16[2,2,16,512]{3,2,1,0:T(8,128)(2,1)S(1)} %join.1.packed_ref), channel_id=1, source_target_pairs={{0,4},{4,0},{1,5},{5,1},{2,6},{6,2},{3,7},{7,3},{8,12},{12,8},{9,1... | collective-permute-start | bytes 196616 | tf_op jit(solution)/shard_map/ppermute | solution.py:291
  22.3 5.7 %collective-permute-start.1 = (bf16[2,2,16,512]{3,2,1,0:T(8,128)(2,1)S(1)}, bf16[2,2,16,512]{3,2,1,0:T(8,128)(2,1)S(1)}, u32[]{:S(2)}, u32[]{:S(2)}) collective-permute-start(bf16[2,2,16,512]{3,2,1,0:T(8,128)(2,1)S(1)} %join.1.packed_ref), channel_id=1, source_target_pairs={{0,24},{8,16},{16,8},{24,0},{1,25},{9,17},{17,9},{25,1},{2,26},{10... | collective-permute-start | bytes 196616 | tf_op jit(solution)/shard_map/ppermute | solution.py:292
  28.0 1.3 %collective-permute-start.3 = (bf16[2,2,16,512]{3,2,1,0:T(8,128)(2,1)S(1)}, bf16[2,2,16,512]{3,2,1,0:T(8,128)(2,1)S(1)}, u32[]{:S(2)}, u32[]{:S(2)}) collective-permute-start(bf16[2,2,16,512]{3,2,1,0:T(8,128)(2,1)S(1)} %after.1.packed_ref), channel_id=1, source_target_pairs={{0,4},{4,0},{1,5},{5,1},{2,6},{6,2},{3,7},{7,3},{8,12},{12,8},{9,1... | collective-permute-start | bytes 196616 | tf_op jit(solution)/shard_map/ppermute | solution.py:306
  39.5 6.8 %collective-permute-start.4 = (bf16[16,512]{1,0:T(8,128)(2,1)S(1)}, bf16[16,512]{1,0:T(8,128)(2,1)S(1)}, u32[]{:S(2)}, u32[]{:S(2)}) collective-permute-start(bf16[16,512]{1,0:T(8,128)(2,1)S(1)} %finish.1), channel_id=1, source_target_pairs={{0,160},{1,0},{2,224},{3,192},{4,164},{5,4},{6,228},{7,196},{8,168... | collective-permute-start | bytes 49160 | tf_op jit(solution)/shard_map/ppermute | solution.py:318

commit v6 on v5

--- a/solution.py
+++ b/solution.py
@@ -11,6 +11,8 @@
 TILES = ZH * ZL
 AXES = ("zh", "zl", "x", "core", "row")
 PIECES = 8
+Z_ORDER = (5, 6, 7, 0, 1, 2, 3, 4)
+GROUP_ORDER = (2, 6, 3, 7, 0, 4, 1, 5)
 TARGETS = (
     (5, 0, 7, 6, 4, 1, 2, 3),
     (1, 0, 7, 2, 5, 6, 3, 4),
@@ -73,8 +75,8 @@
     zh, zl, row = lax.axis_index("zh"), lax.axis_index("zl"), lax.axis_index("row")
     for h in range(2):
         source = partner_ref[2 * row + h]
-        for z in range(TILES):
-            pick_ref[h, z] = jnp.full(pick_ref.shape[2:], jnp.where(source == z, 1, 0), jnp.int32)
+        for place, z in enumerate(Z_ORDER):
+            pick_ref[h, place] = jnp.full(pick_ref.shape[2:], jnp.where(source == z, 1, 0), jnp.int32)
     packed = jnp.where(zh == 0, PACKED_TARGETS[0], PACKED_TARGETS[1])
     packed = jnp.where(zh == 2, PACKED_TARGETS[2], jnp.where(zh == 3, PACKED_TARGETS[3], packed))
     target = lax.shift_right_logical(packed, 3 * (zl * ROW + row)) & (TILES - 1)
@@ -194,9 +196,9 @@
     odd = jnp.concatenate([odd_ref[...]] * (out_ref.shape[1] // odd_ref.shape[1]), axis=1) != 0
     sums = []
     for h in range(2):
-        total = shared_ref[h * ROW]
+        total = shared_ref[GROUP_ORDER.index(h * ROW)]
         for j in range(1, ROW):
-            total = total + shared_ref[h * ROW + j]
+            total = total + shared_ref[GROUP_ORDER.index(h * ROW + j)]
         sums.append(total)
     out_ref[...] = jnp.where(odd, sums[1], sums[0]).astype(out_ref.dtype)
 
@@ -239,7 +241,7 @@
         compiler_params=params,
         name="prepare",
     )(in_hbm(partner), in_hbm(amplitudes))
-    got = lax.all_to_all(sent, ("zh", "zl"), 0, 0, tiled=True)
+    got = lax.all_to_all(sent, ("zh", "zl"), 0, 0, axis_index_groups=[list(Z_ORDER)], tiled=True)
     chosen = pl.pallas_call(
         choose_kernel,
         out_shape=pltpu.VMEM((2, pairs, width), jnp.bfloat16),
@@ -306,7 +308,7 @@
     swapped = lax.ppermute(across, "core", core_swap)
     total = multiply(far_kernel, [across, total, top, bottom], "far_product")
     partials = multiply(last_kernel, [swapped, total, top, bottom], "last_product", (ZL * ROW,))
-    shared = lax.all_to_all(partials, ("zl", "row"), 0, 0, tiled=True)
+    shared = lax.all_to_all(partials, ("zl", "row"), 0, 0, axis_index_groups=[list(GROUP_ORDER)], tiled=True)
     block = pl.pallas_call(
         finish_kernel,
         out_shape=pltpu.VMEM((pairs, bra), jnp.bfloat16),

time: 47.3 us -> 44.1 us (0.932)
  blocking collectives: 26.9 us -> 23.7 us
  starting transfers between devices: 6.46 us -> 8.09 us
  waiting for transfers between devices: 6.17 us -> 4.54 us
    all_to_all x2, blocking collectives: 26.9 us -> 23.7 us  [the longest x1 13.8 us: per_device(): lax.all_to_all(sent, ('zh', 'zl'), 0, 0, axis_index_groups=[list(Z_ORDER)...]
    ppermute x1, starting transfers between devices: 2.03 us -> 3.66 us  [per_device(): block = lax.ppermute(block, AXES, delivery_pairs())]
    ppermute x1, waiting for transfers between devices: 4.79 us -> 3.16 us  [per_device(): block = lax.ppermute(block, AXES, delivery_pairs())]
  transfers between devices with their start and end apart: 5 -> 5, of which waited for: 4 -> 4; matrix products, arithmetic and copies ran while one was open for 0% -> 0% of each run, Pallas kernels for 11% -> 12%
where the time goes in v6:
time: 44.1 us; the launch traced here: 43.9 us
  blocking collectives  23.7 us (54%)
  starting transfers between devices  8.09 us (18%)
  Pallas kernels  7.46 us (17%)
  waiting for transfers between devices  4.54 us (10%)
    all_to_all x1, blocking collectives, per_device(): lax.all_to_all(sent, ('zh', 'zl'), 0, 0, axis_index_groups=[list(Z_ORDER)...  13.8 us
    all_to_all x1, blocking collectives, per_device(): lax.all_to_all(partials, ('zl', 'row'), 0, 0, axis_index_groups=[list(GRO...  9.87 us
    ppermute x1, starting transfers between devices, per_device(): block = lax.ppermute(block, AXES, delivery_pairs())  3.66 us
    ppermute x1, waiting for transfers between devices, per_device(): block = lax.ppermute(block, AXES, delivery_pairs())  3.16 us
    ppermute x1, starting transfers between devices, per_device(): across = lax.ppermute(couple, 'x', [(i, X - 1 - i) for i in range(X)])  2.85 us
    pallas_call x1, Pallas kernels, per_device(): pl.pallas_call(near_kernel, out_shape=[staged, pltpu.VMEM((pairs, bra), j...  2.28 us
    pallas_call x1, Pallas kernels, per_device(): pl.pallas_call(stage_top_kernel, out_shape=staged, in_specs=[HBM], out_sp...  2.21 us
    ppermute x1, starting transfers between devices, per_device(): beside = lax.ppermute(chosen, 'x', [(i, i ^ 1) for i in range(X)])  1.58 us
  transfers between devices with their start and end apart: 5, of which 4 were waited for; matrix products, arithmetic and copies ran while one was open for 0% of the time, Pallas kernels for 12%

profile of v6, /device:TPU:16, one launch (start us, length us, event | category | flops | bytes accessed | tf_op | source)
XLA Modules:
  0.0 43.9 jit_solution(12829061392211242547)
XLA Ops:
  0.0 0.9 %prepare.1 = (bf16[8,16,512]{2,1,0:T(8,128)(2,1)S(1)}, s32[2,8,16,128]{3,2,1,0:T(8,128)S(1)}, s32[16,128]{1,0:T(8,128)S(1)}, s32[2,16,128]{2,1,0:T(8,128)S(1)}) custom-call(s32[8]{0:T(128)} %partner_hbm.1, bf16[16,8,128]{2,1,0:T(8,128)(2,1)} %amplitudes_hbm.1), custom_call_target="tpu_custom_call" | custom-call | tf_op jit(solution)/shard_map/prepare/pallas_call | solution.py:226
  0.9 13.8 %all_to_all.10.got_ref = bf16[8,16,512]{2,1,0:T(8,128)(2,1)S(1)} all-to-all(bf16[8,16,512]{2,1,0:T(8,128)(2,1)S(1)} %get-tuple-element.14), channel_id=1, replica_groups={{160,192,224,0,32,64,96,128},{161,193,225,1,33,65,97,129},{162,194,226,..., dimensions={0} | all-to-all | bytes 262144 | tf_op jit(solution)/shard_map/all_to_all | solution.py:244
  14.8 1.6 %collective-permute-start = (bf16[2,16,512]{2,1,0:T(8,128)(2,1)S(1)}, bf16[2,16,512]{2,1,0:T(8,128)(2,1)S(1)}, u32[]{:S(2)}, u32[]{:S(2)}) collective-permute-start(bf16[2,16,512]{2,1,0:T(8,128)(2,1)S(1)} %choose.1), channel_id=1, source_target_pairs={{0,8},{8,0},{16,24},{24,16},{1,9},{9,1},{17,25},{25,17},{2,10},{10... | collective-permute-start | bytes 98312 | tf_op jit(solution)/shard_map/ppermute | solution.py:275
  16.3 2.2 %stage_top.1.rest_0_.top_ref = bf16[256,8192]{1,0:T(8,128)(2,1)S(1)} custom-call(bf16[512,8192]{1,0:T(8,128)(2,1)} %integrals_ref.3), custom_call_target="tpu_custom_call" | custom-call | bytes 8388608 | tf_op jit(solution)/shard_map/stage_top/pallas_call | solution.py:276
  18.6 0.2 collective-permute-done
  18.8 0.0 collective-permute-start.2
  18.8 2.8 %collective-permute-start.1 = (bf16[2,2,16,512]{3,2,1,0:T(8,128)(2,1)S(1)}, bf16[2,2,16,512]{3,2,1,0:T(8,128)(2,1)S(1)}, u32[]{:S(2)}, u32[]{:S(2)}) collective-permute-start(bf16[2,2,16,512]{3,2,1,0:T(8,128)(2,1)S(1)} %join.1.packed_ref), channel_id=1, source_target_pairs={{0,24},{8,16},{16,8},{24,0},{1,25},{9,17},{17,9},{25,1},{2,26},{10... | collective-permute-start | bytes 196616 | tf_op jit(solution)/shard_map/ppermute | solution.py:294
  21.6 0.0 collective-permute-done.2.swapped_ref
  21.6 2.3 %near_product.1 = (bf16[256,8192]{1,0:T(8,128)(2,1)S(1)}, f32[16,512]{1,0:T(8,128)S(1)}) custom-call(bf16[2,2,16,512]{3,2,1,0:T(8,128)(2,1)S(1)} %join.1.packed_ref, bf16[2,2,16,512]{3,2,1,0:T(8,128)(2,1)S(1)} %collective-permute-done.2.swapped_ref, bf16[256,8192]{1,0:T(8,128)(2,1)S(1)} %stage_top.1.rest_0_.top_ref, bf16[512,8192]{1,0:T(8,128)(2,1)} %integrals_ref.3), custom_call_target="tpu_custom_call" | custom-call | flops 67108864 | bytes 8388608 | tf_op jit(solution)/shard_map/near_product/pallas_call | solution.py:295
  23.9 0.6 %collective-permute-done.1.value_ref = bf16[2,2,16,512]{3,2,1,0:T(8,128)(2,1)S(1)} collective-permute-done((bf16[2,2,16,512]{3,2,1,0:T(8,128)(2,1)S(1)}, bf16[2,2,16,512]{3,2,1,0:T(8,128)(2,1)S(1)}, u32[]{:S(2)}, u32[]{:S(2)}) %collective-permute-start.1) | collective-permute-done | bytes 65568 | tf_op jit(solution)/shard_map/ppermute | solution.py:294
  24.5 0.0 collective-permute-start.3
  24.5 0.7 %far_product.1.before_ref = f32[16,512]{1,0:T(8,128)S(1)} custom-call(bf16[2,2,16,512]{3,2,1,0:T(8,128)(2,1)S(1)} %after.1.packed_ref, f32[16,512]{1,0:T(8,128)S(1)} %get-tuple-element.15.first_ref.before_ref, bf16[256,8192]{1,0:T(8,128)(2,1)S(1)} %stage_top.1.rest_0_.top_ref, bf16[256,8192]{1,0:T(8,128)(2,1)S(1)} %get-tuple-element.16.bottom_ref), custom_call_target="tpu_custom_call" | custom-call | flops 33554432 | bytes 2097152 | tf_op jit(solution)/shard_map/far_product/pallas_call | solution.py:256
  25.2 0.6 %collective-permute-done.3.packed_ref = bf16[2,2,16,512]{3,2,1,0:T(8,128)(2,1)S(1)} collective-permute-done((bf16[2,2,16,512]{3,2,1,0:T(8,128)(2,1)S(1)}, bf16[2,2,16,512]{3,2,1,0:T(8,128)(2,1)S(1)}, u32[]{:S(2)}, u32[]{:S(2)}) %collective-permute-start.3) | collective-permute-done | bytes 65568 | tf_op jit(solution)/shard_map/ppermute | solution.py:308
  25.8 0.7 %last_product.1 = f32[8,16,512]{2,1,0:T(8,128)S(1)} custom-call(bf16[2,2,16,512]{3,2,1,0:T(8,128)(2,1)S(1)} %collective-permute-done.3.packed_ref, f32[16,512]{1,0:T(8,128)S(1)} %far_product.1.before_ref, bf16[256,8192]{1,0:T(8,128)(2,1)S(1)} %stage_top.1.rest_0_.top_ref, bf16[256,8192]{1,0:T(8,128)(2,1)S(1)} %get-tuple-element.16.bottom_ref), custom_call_target="tpu_custom_call" | custom-call | flops 33554432 | bytes 2097152 | tf_op jit(solution)/shard_map/last_product/pallas_call | solution.py:256
  26.4 9.9 %all_to_all.11.shared_ref = f32[8,16,512]{2,1,0:T(8,128)S(1)} all-to-all(f32[8,16,512]{2,1,0:T(8,128)S(1)} %last_product.1), channel_id=1, replica_groups={{2,34,3,35,0,32,1,33},{6,38,7,39,4,36,5,37},{10,42,11,43,8,40,9,41},{14..., dimensions={0} | all-to-all | bytes 524288 | tf_op jit(solution)/shard_map/all_to_all | solution.py:311
  36.3 3.7 %collective-permute-start.4 = (bf16[16,512]{1,0:T(8,128)(2,1)S(1)}, bf16[16,512]{1,0:T(8,128)(2,1)S(1)}, u32[]{:S(2)}, u32[]{:S(2)}) collective-permute-start(bf16[16,512]{1,0:T(8,128)(2,1)S(1)} %finish.1), channel_id=1, source_target_pairs={{0,160},{1,0},{2,224},{3,192},{4,164},{5,4},{6,228},{7,196},{8,168... | collective-permute-start | bytes 49160 | tf_op jit(solution)/shard_map/ppermute | solution.py:320
  40.0 3.2 %collective-permute-done.4.block_ref = bf16[16,512]{1,0:T(8,128)(2,1)S(1)} collective-permute-done((bf16[16,512]{1,0:T(8,128)(2,1)S(1)}, bf16[16,512]{1,0:T(8,128)(2,1)S(1)}, u32[]{:S(2)}, u32[]{:S(2)}) %collective-permute-start.4) | collective-permute-done | bytes 16416 | tf_op jit(solution)/shard_map/ppermute | solution.py:320
  43.2 0.7 %place.1 = bf16[16,8,128]{2,1,0:T(8,128)(2,1)} custom-call(s32[2,16,128]{2,1,0:T(8,128)S(1)} %get-tuple-element.11.place_ref, bf16[16,512]{1,0:T(8,128)(2,1)S(1)} %collective-permute-done.4.block_ref), custom_call_target="tpu_custom_call" | custom-call | tf_op jit(solution)/shard_map/place/pallas_call | solution.py:321
  (4 shorter events, 0.1 us)
Async XLA Ops:
  14.8 4.0 %collective-permute-start = (bf16[2,16,512]{2,1,0:T(8,128)(2,1)S(1)}, bf16[2,16,512]{2,1,0:T(8,128)(2,1)S(1)}, u32[]{:S(2)}, u32[]{:S(2)}) collective-permute-start(bf16[2,16,512]{2,1,0:T(8,128)(2,1)S(1)} %choose.1), channel_id=1, source_target_pairs={{0,8},{8,0},{16,24},{24,16},{1,9},{9,1},{17,25},{25,17},{2,10},{10... | collective-permute-start | bytes 98312 | tf_op jit(solution)/shard_map/ppermute | solution.py:275
  18.8 2.9 %collective-permute-start.2 = (bf16[2,2,16,512]{3,2,1,0:T(8,128)(2,1)S(1)}, bf16[2,2,16,512]{3,2,1,0:T(8,128)(2,1)S(1)}, u32[]{:S(2)}, u32[]{:S(2)}) collective-permute-start(bf16[2,2,16,512]{3,2,1,0:T(8,128)(2,1)S(1)} %join.1.packed_ref), channel_id=1, source_target_pairs={{0,4},{4,0},{1,5},{5,1},{2,6},{6,2},{3,7},{7,3},{8,12},{12,8},{9,1... | collective-permute-start | bytes 196616 | tf_op jit(solution)/shard_map/ppermute | solution.py:293
  18.8 5.7 %collective-permute-start.1 = (bf16[2,2,16,512]{3,2,1,0:T(8,128)(2,1)S(1)}, bf16[2,2,16,512]{3,2,1,0:T(8,128)(2,1)S(1)}, u32[]{:S(2)}, u32[]{:S(2)}) collective-permute-start(bf16[2,2,16,512]{3,2,1,0:T(8,128)(2,1)S(1)} %join.1.packed_ref), channel_id=1, source_target_pairs={{0,24},{8,16},{16,8},{24,0},{1,25},{9,17},{17,9},{25,1},{2,26},{10... | collective-permute-start | bytes 196616 | tf_op jit(solution)/shard_map/ppermute | solution.py:294
  24.5 1.3 %collective-permute-start.3 = (bf16[2,2,16,512]{3,2,1,0:T(8,128)(2,1)S(1)}, bf16[2,2,16,512]{3,2,1,0:T(8,128)(2,1)S(1)}, u32[]{:S(2)}, u32[]{:S(2)}) collective-permute-start(bf16[2,2,16,512]{3,2,1,0:T(8,128)(2,1)S(1)} %after.1.packed_ref), channel_id=1, source_target_pairs={{0,4},{4,0},{1,5},{5,1},{2,6},{6,2},{3,7},{7,3},{8,12},{12,8},{9,1... | collective-permute-start | bytes 196616 | tf_op jit(solution)/shard_map/ppermute | solution.py:308
  36.3 6.8 %collective-permute-start.4 = (bf16[16,512]{1,0:T(8,128)(2,1)S(1)}, bf16[16,512]{1,0:T(8,128)(2,1)S(1)}, u32[]{:S(2)}, u32[]{:S(2)}) collective-permute-start(bf16[16,512]{1,0:T(8,128)(2,1)S(1)} %finish.1), channel_id=1, source_target_pairs={{0,160},{1,0},{2,224},{3,192},{4,164},{5,4},{6,228},{7,196},{8,168... | collective-permute-start | bytes 49160 | tf_op jit(solution)/shard_map/ppermute | solution.py:320

commit v7 on v6

--- a/solution.py
+++ b/solution.py
@@ -11,7 +11,7 @@
 TILES = ZH * ZL
 AXES = ("zh", "zl", "x", "core", "row")
 PIECES = 8
-Z_ORDER = (5, 6, 7, 0, 1, 2, 3, 4)
+Z_ORDER = (5, 4, 6, 7, 0, 1, 2, 3)
 GROUP_ORDER = (2, 6, 3, 7, 0, 4, 1, 5)
 TARGETS = (
     (5, 0, 7, 6, 4, 1, 2, 3),
@@ -128,9 +128,17 @@
     out_ref[...] = value_ref[...]
 
 
+def facing(x):
+    return X - 1 - x
+
+
+def beside(x):
+    return x + 1 - 2 * (x % 2)
+
+
 def partial_product(packed_ref, integrals_ref, core, x):
     width = packed_ref.shape[3]
-    places = [x, x + 1 - 2 * (x % 2)]
+    places = [x, facing(x)]
     total = jnp.zeros((packed_ref.shape[2], integrals_ref.shape[0]), jnp.float32)
     for i, place in enumerate(places):
         for h in range(2):
@@ -151,12 +159,11 @@
 def near_kernel(packed_ref, swapped_ref, top_ref, integrals_ref, bottom_ref, out_ref, sems):
     core, x = lax.axis_index("core"), lax.axis_index("x")
     rows, columns = bottom_ref.shape
-    span = columns // 4
+    span = columns // (2 * X)
     copies = []
-    for n in range(2):
-        pair = (x // 2 + n) % 2
+    for place in (x, facing(x), beside(x), facing(beside(x))):
         for h in range(2):
-            part = pl.ds(pl.multiple_of((2 * h + pair) * span, span), span)
+            part = pl.ds(pl.multiple_of((h * X + place) * span, span), span)
             source = integrals_ref.at[pl.ds(rows, rows), part]
             copy = pltpu.make_async_copy(source, bottom_ref.at[:, part], sems.at[len(copies)])
             copy.start()
@@ -169,24 +176,24 @@
     def _():
         out_ref[:, pl.ds(0, rows)] = both(top_ref)
 
-    for copy in copies[:2]:
+    for copy in copies[:4]:
         copy.wait()
 
     @pl.when(x >= 0)
     def _():
         out_ref[:, pl.ds(rows, rows)] = both(bottom_ref)
 
-    for copy in copies[2:]:
+    for copy in copies[4:]:
         copy.wait()
 
 
 def far_kernel(packed_ref, before_ref, top_ref, bottom_ref, out_ref):
-    core, x = lax.axis_index("core"), X - 1 - lax.axis_index("x")
+    core, x = lax.axis_index("core"), beside(lax.axis_index("x"))
     out_ref[...] = before_ref[...] + product(packed_ref, top_ref, bottom_ref, core, x)
 
 
 def last_kernel(packed_ref, before_ref, top_ref, bottom_ref, out_ref):
-    core, x = 1 - lax.axis_index("core"), X - 1 - lax.axis_index("x")
+    core, x = 1 - lax.axis_index("core"), beside(lax.axis_index("x"))
     total = before_ref[...] + product(packed_ref, top_ref, bottom_ref, core, x)
     for j in range(out_ref.shape[0]):
         out_ref[j] = total
@@ -272,7 +279,7 @@
         return local(kernel, (*copies, pairs, bra), jnp.float32, operands, cost, name)
 
     core_swap = [(0, 1), (1, 0)]
-    beside = lax.ppermute(chosen, "x", [(i, i ^ 1) for i in range(X)])
+    opposite = lax.ppermute(chosen, "x", [(i, facing(i)) for i in range(X)])
     top = pl.pallas_call(
         stage_top_kernel,
         out_shape=staged,
@@ -287,11 +294,11 @@
         join_kernel,
         (2, 2, pairs, width),
         chosen.dtype,
-        [in_vmem(chosen[None]), in_vmem(beside[None]), in_vmem(top)],
+        [in_vmem(chosen[None]), in_vmem(opposite[None]), in_vmem(top)],
         name="join",
     )
     swapped = lax.ppermute(couple, "core", core_swap)
-    across = lax.ppermute(couple, "x", [(i, X - 1 - i) for i in range(X)])
+    across = lax.ppermute(couple, "x", [(i, beside(i)) for i in range(X)])
     bottom, total = pl.pallas_call(
         near_kernel,
         out_shape=[staged, pltpu.VMEM((pairs, bra), jnp.float32)],

time: 44.1 us -> 44 us (level)
  waiting for transfers between devices: 4.54 us -> 5.86 us
  starting transfers between devices: 8.09 us -> 6.78 us
    ppermute x2, starting transfers between devices: 4.42 us -> 3.21 us  [the longest x1 2.85 us: per_device(): opposite = lax.ppermute(chosen, 'x', [(i, facing(i)) for i in range(X)])]
    ppermute x1, waiting for transfers between devices: 0.01 us -> 0.88 us  [per_device(): swapped = lax.ppermute(couple, 'core', core_swap)]
  transfers between devices with their start and end apart: 5 -> 5, of which waited for: 4 -> 5; matrix products, arithmetic and copies ran while one was open for 0% -> 0% of each run, Pallas kernels for 12% -> 12%
where the time goes in v7:
time: 44 us; the launch traced here: 43.8 us
  blocking collectives  23.6 us (54%)
  Pallas kernels  7.44 us (17%)
  starting transfers between devices  6.78 us (15%)
  waiting for transfers between devices  5.86 us (13%)
    all_to_all x1, blocking collectives, per_device(): lax.all_to_all(sent, ('zh', 'zl'), 0, 0, axis_index_groups=[list(Z_ORDER)...  13.7 us
    all_to_all x1, blocking collectives, per_device(): lax.all_to_all(partials, ('zl', 'row'), 0, 0, axis_index_groups=[list(GRO...  9.87 us
    ppermute x1, starting transfers between devices, per_device(): block = lax.ppermute(block, AXES, delivery_pairs())  3.57 us
    ppermute x1, waiting for transfers between devices, per_device(): block = lax.ppermute(block, AXES, delivery_pairs())  3.26 us
    ppermute x1, starting transfers between devices, per_device(): opposite = lax.ppermute(chosen, 'x', [(i, facing(i)) for i in range(X)])  2.85 us
    pallas_call x1, Pallas kernels, per_device(): pl.pallas_call(near_kernel, out_shape=[staged, pltpu.VMEM((pairs, bra), j...  2.26 us
    pallas_call x1, Pallas kernels, per_device(): pl.pallas_call(stage_top_kernel, out_shape=staged, in_specs=[HBM], out_sp...  2.21 us
    pallas_call x4, Pallas kernels, local(): pl.pallas_call(kernel, out_shape=pltpu.VMEM(shape, dtype), in_specs=specs...  1.34 us
  transfers between devices with their start and end apart: 5, of which 5 were waited for; matrix products, arithmetic and copies ran while one was open for 0% of the time, Pallas kernels for 12%

profile of v7, /device:TPU:16, one launch (start us, length us, event | category | flops | bytes accessed | tf_op | source)
XLA Modules:
  0.0 43.8 jit_solution(11482789745476070978)
XLA Ops:
  0.0 0.9 %prepare.1 = (bf16[8,16,512]{2,1,0:T(8,128)(2,1)S(1)}, s32[2,8,16,128]{3,2,1,0:T(8,128)S(1)}, s32[16,128]{1,0:T(8,128)S(1)}, s32[2,16,128]{2,1,0:T(8,128)S(1)}) custom-call(s32[8]{0:T(128)} %partner_hbm.1, bf16[16,8,128]{2,1,0:T(8,128)(2,1)} %amplitudes_hbm.1), custom_call_target="tpu_custom_call" | custom-call | tf_op jit(solution)/shard_map/prepare/pallas_call | solution.py:233
  0.9 13.7 %all_to_all.10.got_ref = bf16[8,16,512]{2,1,0:T(8,128)(2,1)S(1)} all-to-all(bf16[8,16,512]{2,1,0:T(8,128)(2,1)S(1)} %get-tuple-element.14), channel_id=1, replica_groups={{160,128,192,224,0,32,64,96},{161,129,193,225,1,33,65,97},{162,130,194,..., dimensions={0} | all-to-all | bytes 262144 | tf_op jit(solution)/shard_map/all_to_all | solution.py:251
  14.7 2.8 %collective-permute-start = (bf16[2,16,512]{2,1,0:T(8,128)(2,1)S(1)}, bf16[2,16,512]{2,1,0:T(8,128)(2,1)S(1)}, u32[]{:S(2)}, u32[]{:S(2)}) collective-permute-start(bf16[2,16,512]{2,1,0:T(8,128)(2,1)S(1)} %choose.1), channel_id=1, source_target_pairs={{0,24},{8,16},{16,8},{24,0},{1,25},{9,17},{17,9},{25,1},{2,26},{10... | collective-permute-start | bytes 98312 | tf_op jit(solution)/shard_map/ppermute | solution.py:282
  17.5 2.2 %stage_top.1.rest_0_.top_ref = bf16[256,8192]{1,0:T(8,128)(2,1)S(1)} custom-call(bf16[512,8192]{1,0:T(8,128)(2,1)} %integrals_ref.3), custom_call_target="tpu_custom_call" | custom-call | bytes 8388608 | tf_op jit(solution)/shard_map/stage_top/pallas_call | solution.py:283
  19.7 0.1 collective-permute-done
  19.9 0.0 collective-permute-start.2
  19.9 0.4 collective-permute-start.1
  20.3 0.9 %collective-permute-done.2.swapped_ref = bf16[2,2,16,512]{3,2,1,0:T(8,128)(2,1)S(1)} collective-permute-done((bf16[2,2,16,512]{3,2,1,0:T(8,128)(2,1)S(1)}, bf16[2,2,16,512]{3,2,1,0:T(8,128)(2,1)S(1)}, u32[]{:S(2)}, u32[]{:S(2)}) %collective-permute-start.2) | collective-permute-done | bytes 65568 | tf_op jit(solution)/shard_map/ppermute | solution.py:300
  21.1 2.3 %near_product.1 = (bf16[256,8192]{1,0:T(8,128)(2,1)S(1)}, f32[16,512]{1,0:T(8,128)S(1)}) custom-call(bf16[2,2,16,512]{3,2,1,0:T(8,128)(2,1)S(1)} %join.1.packed_ref, bf16[2,2,16,512]{3,2,1,0:T(8,128)(2,1)S(1)} %collective-permute-done.2.swapped_ref, bf16[256,8192]{1,0:T(8,128)(2,1)S(1)} %stage_top.1.rest_0_.top_ref, bf16[512,8192]{1,0:T(8,128)(2,1)} %integrals_ref.3), custom_call_target="tpu_custom_call" | custom-call | flops 67108864 | bytes 8388608 | tf_op jit(solution)/shard_map/near_product/pallas_call | solution.py:302
  23.4 1.0 %collective-permute-done.1.value_ref = bf16[2,2,16,512]{3,2,1,0:T(8,128)(2,1)S(1)} collective-permute-done((bf16[2,2,16,512]{3,2,1,0:T(8,128)(2,1)S(1)}, bf16[2,2,16,512]{3,2,1,0:T(8,128)(2,1)S(1)}, u32[]{:S(2)}, u32[]{:S(2)}) %collective-permute-start.1) | collective-permute-done | bytes 65568 | tf_op jit(solution)/shard_map/ppermute | solution.py:301
  24.4 0.0 collective-permute-start.3
  24.4 0.7 %far_product.1.before_ref = f32[16,512]{1,0:T(8,128)S(1)} custom-call(bf16[2,2,16,512]{3,2,1,0:T(8,128)(2,1)S(1)} %after.1.packed_ref, f32[16,512]{1,0:T(8,128)S(1)} %get-tuple-element.15.first_ref.before_ref, bf16[256,8192]{1,0:T(8,128)(2,1)S(1)} %stage_top.1.rest_0_.top_ref, bf16[256,8192]{1,0:T(8,128)(2,1)S(1)} %get-tuple-element.16.bottom_ref), custom_call_target="tpu_custom_call" | custom-call | flops 33554432 | bytes 2097152 | tf_op jit(solution)/shard_map/far_product/pallas_call | solution.py:263
  25.1 0.6 %collective-permute-done.3.packed_ref = bf16[2,2,16,512]{3,2,1,0:T(8,128)(2,1)S(1)} collective-permute-done((bf16[2,2,16,512]{3,2,1,0:T(8,128)(2,1)S(1)}, bf16[2,2,16,512]{3,2,1,0:T(8,128)(2,1)S(1)}, u32[]{:S(2)}, u32[]{:S(2)}) %collective-permute-start.3) | collective-permute-done | bytes 65568 | tf_op jit(solution)/shard_map/ppermute | solution.py:315
  25.7 0.7 %last_product.1 = f32[8,16,512]{2,1,0:T(8,128)S(1)} custom-call(bf16[2,2,16,512]{3,2,1,0:T(8,128)(2,1)S(1)} %collective-permute-done.3.packed_ref, f32[16,512]{1,0:T(8,128)S(1)} %far_product.1.before_ref, bf16[256,8192]{1,0:T(8,128)(2,1)S(1)} %stage_top.1.rest_0_.top_ref, bf16[256,8192]{1,0:T(8,128)(2,1)S(1)} %get-tuple-element.16.bottom_ref), custom_call_target="tpu_custom_call" | custom-call | flops 33554432 | bytes 2097152 | tf_op jit(solution)/shard_map/last_product/pallas_call | solution.py:263
  26.3 9.9 %all_to_all.11.shared_ref = f32[8,16,512]{2,1,0:T(8,128)S(1)} all-to-all(f32[8,16,512]{2,1,0:T(8,128)S(1)} %last_product.1), channel_id=1, replica_groups={{2,34,3,35,0,32,1,33},{6,38,7,39,4,36,5,37},{10,42,11,43,8,40,9,41},{14..., dimensions={0} | all-to-all | bytes 524288 | tf_op jit(solution)/shard_map/all_to_all | solution.py:318
  36.2 3.6 %collective-permute-start.4 = (bf16[16,512]{1,0:T(8,128)(2,1)S(1)}, bf16[16,512]{1,0:T(8,128)(2,1)S(1)}, u32[]{:S(2)}, u32[]{:S(2)}) collective-permute-start(bf16[16,512]{1,0:T(8,128)(2,1)S(1)} %finish.1), channel_id=1, source_target_pairs={{0,160},{1,0},{2,224},{3,192},{4,164},{5,4},{6,228},{7,196},{8,168... | collective-permute-start | bytes 49160 | tf_op jit(solution)/shard_map/ppermute | solution.py:327
  39.8 3.3 %collective-permute-done.4.block_ref = bf16[16,512]{1,0:T(8,128)(2,1)S(1)} collective-permute-done((bf16[16,512]{1,0:T(8,128)(2,1)S(1)}, bf16[16,512]{1,0:T(8,128)(2,1)S(1)}, u32[]{:S(2)}, u32[]{:S(2)}) %collective-permute-start.4) | collective-permute-done | bytes 16416 | tf_op jit(solution)/shard_map/ppermute | solution.py:327
  43.1 0.7 %place.1 = bf16[16,8,128]{2,1,0:T(8,128)(2,1)} custom-call(s32[2,16,128]{2,1,0:T(8,128)S(1)} %get-tuple-element.11.place_ref, bf16[16,512]{1,0:T(8,128)(2,1)S(1)} %collective-permute-done.4.block_ref), custom_call_target="tpu_custom_call" | custom-call | tf_op jit(solution)/shard_map/place/pallas_call | solution.py:328
  (4 shorter events, 0.1 us)
Async XLA Ops:
  14.7 5.2 %collective-permute-start = (bf16[2,16,512]{2,1,0:T(8,128)(2,1)S(1)}, bf16[2,16,512]{2,1,0:T(8,128)(2,1)S(1)}, u32[]{:S(2)}, u32[]{:S(2)}) collective-permute-start(bf16[2,16,512]{2,1,0:T(8,128)(2,1)S(1)} %choose.1), channel_id=1, source_target_pairs={{0,24},{8,16},{16,8},{24,0},{1,25},{9,17},{17,9},{25,1},{2,26},{10... | collective-permute-start | bytes 98312 | tf_op jit(solution)/shard_map/ppermute | solution.py:282
  19.9 1.3 %collective-permute-start.2 = (bf16[2,2,16,512]{3,2,1,0:T(8,128)(2,1)S(1)}, bf16[2,2,16,512]{3,2,1,0:T(8,128)(2,1)S(1)}, u32[]{:S(2)}, u32[]{:S(2)}) collective-permute-start(bf16[2,2,16,512]{3,2,1,0:T(8,128)(2,1)S(1)} %join.1.packed_ref), channel_id=1, source_target_pairs={{0,4},{4,0},{1,5},{5,1},{2,6},{6,2},{3,7},{7,3},{8,12},{12,8},{9,1... | collective-permute-start | bytes 196616 | tf_op jit(solution)/shard_map/ppermute | solution.py:300
  19.9 4.5 %collective-permute-start.1 = (bf16[2,2,16,512]{3,2,1,0:T(8,128)(2,1)S(1)}, bf16[2,2,16,512]{3,2,1,0:T(8,128)(2,1)S(1)}, u32[]{:S(2)}, u32[]{:S(2)}) collective-permute-start(bf16[2,2,16,512]{3,2,1,0:T(8,128)(2,1)S(1)} %join.1.packed_ref), channel_id=1, source_target_pairs={{0,8},{8,0},{16,24},{24,16},{1,9},{9,1},{17,25},{25,17},{2,10},{10... | collective-permute-start | bytes 196616 | tf_op jit(solution)/shard_map/ppermute | solution.py:301
  24.4 1.3 %collective-permute-start.3 = (bf16[2,2,16,512]{3,2,1,0:T(8,128)(2,1)S(1)}, bf16[2,2,16,512]{3,2,1,0:T(8,128)(2,1)S(1)}, u32[]{:S(2)}, u32[]{:S(2)}) collective-permute-start(bf16[2,2,16,512]{3,2,1,0:T(8,128)(2,1)S(1)} %after.1.packed_ref), channel_id=1, source_target_pairs={{0,4},{4,0},{1,5},{5,1},{2,6},{6,2},{3,7},{7,3},{8,12},{12,8},{9,1... | collective-permute-start | bytes 196616 | tf_op jit(solution)/shard_map/ppermute | solution.py:315
  36.2 6.8 %collective-permute-start.4 = (bf16[16,512]{1,0:T(8,128)(2,1)S(1)}, bf16[16,512]{1,0:T(8,128)(2,1)S(1)}, u32[]{:S(2)}, u32[]{:S(2)}) collective-permute-start(bf16[16,512]{1,0:T(8,128)(2,1)S(1)} %finish.1), channel_id=1, source_target_pairs={{0,160},{1,0},{2,224},{3,192},{4,164},{5,4},{6,228},{7,196},{8,168... | collective-permute-start | bytes 49160 | tf_op jit(solution)/shard_map/ppermute | solution.py:327

commit v8 on v6

--- a/solution.py
+++ b/solution.py
@@ -11,7 +11,7 @@
 TILES = ZH * ZL
 AXES = ("zh", "zl", "x", "core", "row")
 PIECES = 8
-Z_ORDER = (5, 6, 7, 0, 1, 2, 3, 4)
+Z_ORDER = (5, 4, 6, 7, 0, 1, 2, 3)
 GROUP_ORDER = (2, 6, 3, 7, 0, 4, 1, 5)
 TARGETS = (
     (5, 0, 7, 6, 4, 1, 2, 3),
@@ -66,12 +66,13 @@
 def prepare_kernel(
     partner_hbm, amplitudes_hbm, sent_ref, pick_ref, odd_ref, place_ref, partner_ref, amplitudes_ref, sems
 ):
-    fetch(
-        [
-            pltpu.make_async_copy(partner_hbm, partner_ref, sems.at[0]),
-            pltpu.make_async_copy(amplitudes_hbm, amplitudes_ref, sems.at[1]),
-        ]
-    )
+    copies = [
+        pltpu.make_async_copy(partner_hbm, partner_ref, sems.at[0]),
+        pltpu.make_async_copy(amplitudes_hbm, amplitudes_ref, sems.at[1]),
+    ]
+    for copy in copies:
+        copy.start()
+    copies[0].wait()
     zh, zl, row = lax.axis_index("zh"), lax.axis_index("zl"), lax.axis_index("row")
     for h in range(2):
         source = partner_ref[2 * row + h]
@@ -86,6 +87,7 @@
     for h in range(2):
         place_ref[h] = jnp.full(place_ref.shape[1:], jnp.where(partner_ref[z] == 2 * row + h, 1, 0), jnp.int32)
     upper = partner_ref[z] % 2 == 1
+    copies[1].wait()
     rows = jnp.swapaxes(amplitudes_ref[...].astype(jnp.float32), 0, 1)
     units, pairs, _ = rows.shape
     lower = lower_lanes(pairs)

time: 44.1 us -> 44 us (level)
  no operation moved by 1% of the time
where the time goes in v8:
time: 44 us; the launch traced here: 43.8 us
  blocking collectives  23.6 us (54%)
  starting transfers between devices  8 us (18%)
  Pallas kernels  7.46 us (17%)
  waiting for transfers between devices  4.64 us (11%)
    all_to_all x1, blocking collectives, per_device(): lax.all_to_all(sent, ('zh', 'zl'), 0, 0, axis_index_groups=[list(Z_ORDER)...  13.7 us
    all_to_all x1, blocking collectives, per_device(): lax.all_to_all(partials, ('zl', 'row'), 0, 0, axis_index_groups=[list(GRO...  9.87 us
    ppermute x1, starting transfers between devices, per_device(): block = lax.ppermute(block, AXES, delivery_pairs())  3.57 us
    ppermute x1, waiting for transfers between devices, per_device(): block = lax.ppermute(block, AXES, delivery_pairs())  3.26 us
    ppermute x1, starting transfers between devices, per_device(): across = lax.ppermute(couple, 'x', [(i, X - 1 - i) for i in range(X)])  2.85 us
    pallas_call x1, Pallas kernels, per_device(): pl.pallas_call(near_kernel, out_shape=[staged, pltpu.VMEM((pairs, bra), j...  2.28 us
    pallas_call x1, Pallas kernels, per_device(): pl.pallas_call(stage_top_kernel, out_shape=staged, in_specs=[HBM], out_sp...  2.21 us
    ppermute x1, starting transfers between devices, per_device(): beside = lax.ppermute(chosen, 'x', [(i, i ^ 1) for i in range(X)])  1.58 us
  transfers between devices with their start and end apart: 5, of which 4 were waited for; matrix products, arithmetic and copies ran while one was open for 0% of the time, Pallas kernels for 12%

profile of v8, /device:TPU:16, one launch (start us, length us, event | category | flops | bytes accessed | tf_op | source)
XLA Modules:
  0.0 43.8 jit_solution(13174822597907918443)
XLA Ops:
  0.0 0.9 %prepare.1 = (bf16[8,16,512]{2,1,0:T(8,128)(2,1)S(1)}, s32[2,8,16,128]{3,2,1,0:T(8,128)S(1)}, s32[16,128]{1,0:T(8,128)S(1)}, s32[2,16,128]{2,1,0:T(8,128)S(1)}) custom-call(s32[8]{0:T(128)} %partner_hbm.1, bf16[16,8,128]{2,1,0:T(8,128)(2,1)} %amplitudes_hbm.1), custom_call_target="tpu_custom_call" | custom-call | tf_op jit(solution)/shard_map/prepare/pallas_call | solution.py:228
  0.9 13.7 %all_to_all.10.got_ref = bf16[8,16,512]{2,1,0:T(8,128)(2,1)S(1)} all-to-all(bf16[8,16,512]{2,1,0:T(8,128)(2,1)S(1)} %get-tuple-element.14), channel_id=1, replica_groups={{160,128,192,224,0,32,64,96},{161,129,193,225,1,33,65,97},{162,130,194,..., dimensions={0} | all-to-all | bytes 262144 | tf_op jit(solution)/shard_map/all_to_all | solution.py:246
  14.7 1.6 %collective-permute-start = (bf16[2,16,512]{2,1,0:T(8,128)(2,1)S(1)}, bf16[2,16,512]{2,1,0:T(8,128)(2,1)S(1)}, u32[]{:S(2)}, u32[]{:S(2)}) collective-permute-start(bf16[2,16,512]{2,1,0:T(8,128)(2,1)S(1)} %choose.1), channel_id=1, source_target_pairs={{0,8},{8,0},{16,24},{24,16},{1,9},{9,1},{17,25},{25,17},{2,10},{10... | collective-permute-start | bytes 98312 | tf_op jit(solution)/shard_map/ppermute | solution.py:277
  16.2 2.2 %stage_top.1.rest_0_.top_ref = bf16[256,8192]{1,0:T(8,128)(2,1)S(1)} custom-call(bf16[512,8192]{1,0:T(8,128)(2,1)} %integrals_ref.3), custom_call_target="tpu_custom_call" | custom-call | bytes 8388608 | tf_op jit(solution)/shard_map/stage_top/pallas_call | solution.py:278
  18.5 0.2 collective-permute-done
  18.7 0.0 collective-permute-start.2
  18.7 2.8 %collective-permute-start.1 = (bf16[2,2,16,512]{3,2,1,0:T(8,128)(2,1)S(1)}, bf16[2,2,16,512]{3,2,1,0:T(8,128)(2,1)S(1)}, u32[]{:S(2)}, u32[]{:S(2)}) collective-permute-start(bf16[2,2,16,512]{3,2,1,0:T(8,128)(2,1)S(1)} %join.1.packed_ref), channel_id=1, source_target_pairs={{0,24},{8,16},{16,8},{24,0},{1,25},{9,17},{17,9},{25,1},{2,26},{10... | collective-permute-start | bytes 196616 | tf_op jit(solution)/shard_map/ppermute | solution.py:296
  21.5 0.0 collective-permute-done.2.swapped_ref
  21.5 2.3 %near_product.1 = (bf16[256,8192]{1,0:T(8,128)(2,1)S(1)}, f32[16,512]{1,0:T(8,128)S(1)}) custom-call(bf16[2,2,16,512]{3,2,1,0:T(8,128)(2,1)S(1)} %join.1.packed_ref, bf16[2,2,16,512]{3,2,1,0:T(8,128)(2,1)S(1)} %collective-permute-done.2.swapped_ref, bf16[256,8192]{1,0:T(8,128)(2,1)S(1)} %stage_top.1.rest_0_.top_ref, bf16[512,8192]{1,0:T(8,128)(2,1)} %integrals_ref.3), custom_call_target="tpu_custom_call" | custom-call | flops 67108864 | bytes 8388608 | tf_op jit(solution)/shard_map/near_product/pallas_call | solution.py:297
  23.8 0.6 %collective-permute-done.1.value_ref = bf16[2,2,16,512]{3,2,1,0:T(8,128)(2,1)S(1)} collective-permute-done((bf16[2,2,16,512]{3,2,1,0:T(8,128)(2,1)S(1)}, bf16[2,2,16,512]{3,2,1,0:T(8,128)(2,1)S(1)}, u32[]{:S(2)}, u32[]{:S(2)}) %collective-permute-start.1) | collective-permute-done | bytes 65568 | tf_op jit(solution)/shard_map/ppermute | solution.py:296
  24.4 0.0 collective-permute-start.3
  24.4 0.7 %far_product.1.before_ref = f32[16,512]{1,0:T(8,128)S(1)} custom-call(bf16[2,2,16,512]{3,2,1,0:T(8,128)(2,1)S(1)} %after.1.packed_ref, f32[16,512]{1,0:T(8,128)S(1)} %get-tuple-element.15.first_ref.before_ref, bf16[256,8192]{1,0:T(8,128)(2,1)S(1)} %stage_top.1.rest_0_.top_ref, bf16[256,8192]{1,0:T(8,128)(2,1)S(1)} %get-tuple-element.16.bottom_ref), custom_call_target="tpu_custom_call" | custom-call | flops 33554432 | bytes 2097152 | tf_op jit(solution)/shard_map/far_product/pallas_call | solution.py:258
  25.1 0.6 %collective-permute-done.3.packed_ref = bf16[2,2,16,512]{3,2,1,0:T(8,128)(2,1)S(1)} collective-permute-done((bf16[2,2,16,512]{3,2,1,0:T(8,128)(2,1)S(1)}, bf16[2,2,16,512]{3,2,1,0:T(8,128)(2,1)S(1)}, u32[]{:S(2)}, u32[]{:S(2)}) %collective-permute-start.3) | collective-permute-done | bytes 65568 | tf_op jit(solution)/shard_map/ppermute | solution.py:310
  25.7 0.7 %last_product.1 = f32[8,16,512]{2,1,0:T(8,128)S(1)} custom-call(bf16[2,2,16,512]{3,2,1,0:T(8,128)(2,1)S(1)} %collective-permute-done.3.packed_ref, f32[16,512]{1,0:T(8,128)S(1)} %far_product.1.before_ref, bf16[256,8192]{1,0:T(8,128)(2,1)S(1)} %stage_top.1.rest_0_.top_ref, bf16[256,8192]{1,0:T(8,128)(2,1)S(1)} %get-tuple-element.16.bottom_ref), custom_call_target="tpu_custom_call" | custom-call | flops 33554432 | bytes 2097152 | tf_op jit(solution)/shard_map/last_product/pallas_call | solution.py:258
  26.3 9.9 %all_to_all.11.shared_ref = f32[8,16,512]{2,1,0:T(8,128)S(1)} all-to-all(f32[8,16,512]{2,1,0:T(8,128)S(1)} %last_product.1), channel_id=1, replica_groups={{2,34,3,35,0,32,1,33},{6,38,7,39,4,36,5,37},{10,42,11,43,8,40,9,41},{14..., dimensions={0} | all-to-all | bytes 524288 | tf_op jit(solution)/shard_map/all_to_all | solution.py:313
  36.2 3.6 %collective-permute-start.4 = (bf16[16,512]{1,0:T(8,128)(2,1)S(1)}, bf16[16,512]{1,0:T(8,128)(2,1)S(1)}, u32[]{:S(2)}, u32[]{:S(2)}) collective-permute-start(bf16[16,512]{1,0:T(8,128)(2,1)S(1)} %finish.1), channel_id=1, source_target_pairs={{0,160},{1,0},{2,224},{3,192},{4,164},{5,4},{6,228},{7,196},{8,168... | collective-permute-start | bytes 49160 | tf_op jit(solution)/shard_map/ppermute | solution.py:322
  39.8 3.3 %collective-permute-done.4.block_ref = bf16[16,512]{1,0:T(8,128)(2,1)S(1)} collective-permute-done((bf16[16,512]{1,0:T(8,128)(2,1)S(1)}, bf16[16,512]{1,0:T(8,128)(2,1)S(1)}, u32[]{:S(2)}, u32[]{:S(2)}) %collective-permute-start.4) | collective-permute-done | bytes 16416 | tf_op jit(solution)/shard_map/ppermute | solution.py:322
  43.1 0.7 %place.1 = bf16[16,8,128]{2,1,0:T(8,128)(2,1)} custom-call(s32[2,16,128]{2,1,0:T(8,128)S(1)} %get-tuple-element.11.place_ref, bf16[16,512]{1,0:T(8,128)(2,1)S(1)} %collective-permute-done.4.block_ref), custom_call_target="tpu_custom_call" | custom-call | tf_op jit(solution)/shard_map/place/pallas_call | solution.py:323
  (4 shorter events, 0.1 us)
Async XLA Ops:
  14.7 4.0 %collective-permute-start = (bf16[2,16,512]{2,1,0:T(8,128)(2,1)S(1)}, bf16[2,16,512]{2,1,0:T(8,128)(2,1)S(1)}, u32[]{:S(2)}, u32[]{:S(2)}) collective-permute-start(bf16[2,16,512]{2,1,0:T(8,128)(2,1)S(1)} %choose.1), channel_id=1, source_target_pairs={{0,8},{8,0},{16,24},{24,16},{1,9},{9,1},{17,25},{25,17},{2,10},{10... | collective-permute-start | bytes 98312 | tf_op jit(solution)/shard_map/ppermute | solution.py:277
  18.7 2.9 %collective-permute-start.2 = (bf16[2,2,16,512]{3,2,1,0:T(8,128)(2,1)S(1)}, bf16[2,2,16,512]{3,2,1,0:T(8,128)(2,1)S(1)}, u32[]{:S(2)}, u32[]{:S(2)}) collective-permute-start(bf16[2,2,16,512]{3,2,1,0:T(8,128)(2,1)S(1)} %join.1.packed_ref), channel_id=1, source_target_pairs={{0,4},{4,0},{1,5},{5,1},{2,6},{6,2},{3,7},{7,3},{8,12},{12,8},{9,1... | collective-permute-start | bytes 196616 | tf_op jit(solution)/shard_map/ppermute | solution.py:295
  18.7 5.7 %collective-permute-start.1 = (bf16[2,2,16,512]{3,2,1,0:T(8,128)(2,1)S(1)}, bf16[2,2,16,512]{3,2,1,0:T(8,128)(2,1)S(1)}, u32[]{:S(2)}, u32[]{:S(2)}) collective-permute-start(bf16[2,2,16,512]{3,2,1,0:T(8,128)(2,1)S(1)} %join.1.packed_ref), channel_id=1, source_target_pairs={{0,24},{8,16},{16,8},{24,0},{1,25},{9,17},{17,9},{25,1},{2,26},{10... | collective-permute-start | bytes 196616 | tf_op jit(solution)/shard_map/ppermute | solution.py:296
  24.4 1.3 %collective-permute-start.3 = (bf16[2,2,16,512]{3,2,1,0:T(8,128)(2,1)S(1)}, bf16[2,2,16,512]{3,2,1,0:T(8,128)(2,1)S(1)}, u32[]{:S(2)}, u32[]{:S(2)}) collective-permute-start(bf16[2,2,16,512]{3,2,1,0:T(8,128)(2,1)S(1)} %after.1.packed_ref), channel_id=1, source_target_pairs={{0,4},{4,0},{1,5},{5,1},{2,6},{6,2},{3,7},{7,3},{8,12},{12,8},{9,1... | collective-permute-start | bytes 196616 | tf_op jit(solution)/shard_map/ppermute | solution.py:310
  36.2 6.8 %collective-permute-start.4 = (bf16[16,512]{1,0:T(8,128)(2,1)S(1)}, bf16[16,512]{1,0:T(8,128)(2,1)S(1)}, u32[]{:S(2)}, u32[]{:S(2)}) collective-permute-start(bf16[16,512]{1,0:T(8,128)(2,1)S(1)} %finish.1), channel_id=1, source_target_pairs={{0,160},{1,0},{2,224},{3,192},{4,164},{5,4},{6,228},{7,196},{8,168... | collective-permute-start | bytes 49160 | tf_op jit(solution)/shard_map/ppermute | solution.py:322
